TPU v7x, 512 devices: a whole 4x8x8 slice. The times are simulated.
512 devices in a mesh: dp: 32 (over y, x), expert: 16 (over z, core).
Axes of the slice: x: 4, y: 8, z: 8, core: 2. Of those that a mesh axis runs over, the one named last changes fastest.
Arguments:
- grad_out: bfloat16 [4096, 3072], P(('dp', 'expert')), may hold values from -6 to 6
- routes: int32 [4096, 4], P(('dp', 'expert')), may hold values from 0 to 15, all different within a row; in each aligned block of 8 rows (0 to 7, 8 to 15, ...) at most 4 rows name the same one
- probs: bfloat16 [4096, 4], P(('dp', 'expert')), may hold values from 0.049804688 to 1
- hidden: bfloat16 [32, 16, 16, 4, 5376], P('dp', 'expert'), may hold values from -6 to 6
- w_down: bfloat16 [16, 5376, 3072], P('expert', 'dp'), may hold values from -0.078125 to 0.078125
Outputs:
- d_probs: float32 [4096, 4], P(('dp', 'expert'))
- d_hidden: bfloat16 [32, 16, 16, 4, 5376], P('dp', 'expert')
- d_down: float32 [16, 5376, 3072], P('expert', 'dp')
Inputs may be any that keep to these rules, and one draw needn't show every extreme that they name: `routes`: each row names 4 different experts; among the rows of one device no expert is named more than 4 times, and exactly 4 times in some device.
All inputs are finite; a program needn't handle non-finite values.
Results may differ from a plain program's by a relative error of at most 0.0029.
Values may be sent and summed in bfloat16 or wider, within the bound.
No kernel may reach another device: no remote copies, remote signals or barrier semaphores. Data moves between devices by JAX's collectives and lax.ppermute only.
A program may use at most 64 MiB of HBM per device.

v0:
```python
import jax
import jax.numpy as jnp
from jax import lax
from jax.sharding import PartitionSpec as P


def body(grad_out, routes, probs, hidden, w_down):
    tok = grad_out.shape[0]
    topk = routes.shape[1]
    width = grad_out.shape[1]
    cap = hidden.shape[3]
    feat = hidden.shape[4]
    nexp = lax.axis_size("expert")
    rows = nexp * cap
    flat = routes.reshape(-1)
    onehot = (flat[:, None] == jnp.arange(nexp, dtype=jnp.int32)[None, :]).astype(jnp.int32)
    before = jnp.cumsum(onehot, axis=0) - onehot
    slot = jnp.sum(before * onehot, axis=1)
    target = flat * cap + slot
    select = target[:, None] == jnp.arange(rows, dtype=jnp.int32)[None, :]
    sel_tok = jnp.sum(select.reshape(tok, topk, rows).astype(jnp.float32), axis=1).astype(
        jnp.bfloat16
    )
    dy_buf = jnp.dot(sel_tok.T, grad_out, preferred_element_type=jnp.float32).astype(jnp.bfloat16)
    p_buf = jnp.sum(
        jnp.where(select, probs.reshape(-1)[:, None].astype(jnp.float32), 0.0), axis=0
    ).astype(jnp.bfloat16)
    recv_dy, recv_p = (
        lax.all_to_all(
            dy_buf.reshape(nexp, cap, width), "expert", split_axis=0, concat_axis=0, tiled=True
        ),
        lax.all_to_all(p_buf.reshape(nexp, cap), "expert", split_axis=0, concat_axis=0, tiled=True),
    )
    dy_rows = recv_dy.reshape(rows, width)
    p_rows = recv_p.reshape(rows)
    h_rows = hidden.reshape(rows, feat)
    h_cols = lax.all_to_all(h_rows, "dp", split_axis=1, concat_axis=0, tiled=True)
    w_local = w_down.reshape(-1, width)
    dy_all, p_all = (
        lax.all_gather(dy_rows, "dp", axis=0, tiled=True),
        lax.all_gather(p_rows, "dp", axis=0, tiled=True),
    )
    u = lax.dot_general(
        dy_all, w_local, (((1,), (1,)), ((), ())), preferred_element_type=jnp.float32
    )
    p_wide = p_all.astype(jnp.float32)[:, None]
    dh_cols = (p_wide * u).astype(jnp.bfloat16)
    partial_value = jnp.sum(h_cols.astype(jnp.float32) * u, axis=1)
    g_all = (p_wide * dy_all.astype(jnp.float32)).astype(jnp.bfloat16)
    d_down = lax.dot_general(
        h_cols, g_all, (((0,), (0,)), ((), ())), preferred_element_type=jnp.float32
    )
    d_hid_rows = lax.all_to_all(dh_cols, "dp", split_axis=0, concat_axis=1, tiled=True)
    d_slot = lax.psum_scatter(partial_value, "dp", scatter_dimension=0, tiled=True)
    returned = lax.all_to_all(
        d_slot.reshape(nexp, cap), "expert", split_axis=0, concat_axis=0, tiled=True
    )
    d_probs = jnp.sum(jnp.where(select, returned.reshape(-1)[None, :], 0.0), axis=1).reshape(
        tok, topk
    )
    return (d_probs, d_hid_rows.reshape(hidden.shape), d_down.reshape(w_down.shape))


def solution(mesh):
    in_specs = (
        P(("dp", "expert"), None),
        P(("dp", "expert"), None),
        P(("dp", "expert"), None),
        P("dp", "expert", None, None, None),
        P("expert", "dp", None),
    )
    out_specs = (
        P(("dp", "expert"), None),
        P("dp", "expert", None, None, None),
        P("expert", "dp", None),
    )
    return jax.shard_map(body, mesh=mesh, in_specs=in_specs, out_specs=out_specs, check_vma=False)
```

profile of v0, /device:TPU:6, one launch (start us, length us, event | category | flops | bytes accessed | tf_op | source)
XLA Modules:
  0.0 391.5 jit_solution(1218274359026280071)
XLA Ops:
  7.2 0.0 all-gather.2.cloned.1.call-start
  7.2 0.8 copy.39
  8.1 0.1 reshape.90
  8.1 0.1 fusion.5
  8.2 0.1 reduce_window_sum.11
  8.3 0.2 select_reduce_fusion.2
  8.5 0.1 reduce_sum.48
  8.5 0.1 copy.43
  8.6 0.1 convert_reduce_fusion
  8.7 1.1 convolution_convert_fusion
  9.8 0.1 reshape.91
  10.0 23.9 %all_to_all.55 = bf16[16,4,3072]{2,1,0:T(4,128)(2,1)S(1)} all-to-all(bf16[16,4,3072]{2,1,0:T(4,128)(2,1)S(1)} %reshape.91), channel_id=1, replica_groups=mesh['dp'=32,'expert'=16] {'expert'}, dimensions={0} | all-to-all | bytes 786432 | tf_op jit(solution)/shard_map/all_to_all | solution.py:29
  33.9 0.8 reshape.92
  34.7 0.0 all-gather.2.cloned.1.call-update
  34.7 4.1 %all_to_all.39 = bf16[64,32,168]{2,1,0:T(8,128)(2,1)S(1)} reshape(bf16[1,1,16,4,5376]{4,3,2,1,0:T(4,128)(2,1)} %param.8) | data formatting | bytes 1376256 | tf_op jit(solution)/shard_map/all_to_all | solution.py:37
  38.9 1.6 copy.40
  40.5 10.3 %all-to-all-start = ((bf16[64,32,168]{2,0,1:T(8,128)(2,1)}), bf16[64,32,168]{2,0,1:T(8,128)(2,1)S(1)}, u32[]{:S(2)}, u32[]{:S(2)}) async-start(bf16[64,32,168]{2,0,1:T(8,128)(2,1)} %copy.40), calls=%async_computation | async-start | bytes 2097152 | tf_op jit(solution)/shard_map/all_to_all | solution.py:37
  50.8 1.4 fusion.7
  52.8 37.5 %all-to-all-done = bf16[64,32,168]{2,0,1:T(8,128)(2,1)S(1)} async-done(((bf16[64,32,168]{2,0,1:T(8,128)(2,1)}), bf16[64,32,168]{2,0,1:T(8,128)(2,1)S(1)}, u32[]{:S(2)}, u32[]{:S(2)}) %all-to-all-start) | async-done | bytes 688160 | tf_op jit(solution)/shard_map/all_to_all | solution.py:37
  90.3 0.5 copy.41
  90.8 78.1 %all-gather.2.cloned.1.call-done = bf16[2048,3072]{1,0:T(8,128)(2,1)} async-done(((bf16[64,3072]{1,0:T(8,128)(2,1)}), bf16[2048,3072]{1,0:T(8,128)(2,1)}) %all-gather.2.cloned.1.call-update) | async-done | bytes 12582928 | tf_op jit(solution)/shard_map/all_gather | solution.py:40
  168.9 10.0 %multiply_reduce_fusion = (f32[2048]{0:T(1024)S(1)}, f32[2048,168]{0,1:T(8,128)}) fusion(bf16[2048,168]{0,1:T(8,128)(2,1)S(1)} %copy.41, bf16[2048,3072]{1,0:T(8,128)(2,1)} %all-gather.2.cloned.1.call-done, bf16[1,168,3072]{2,1,0:T(8,128)(2,1)S(1)} %copy-done), kind=kOutput, calls=%fused_computation.6 | convolution fusion | flops 2114959360 | bytes 15687680 | tf_op jit(solution)/shard_map/dot_general | solution.py:43
  178.9 69.1 %all-reduce.1 = f32[2048]{0:T(1024)S(1)} all-reduce(f32[2048]{0:T(1024)S(1)} %get-tuple-element.22), channel_id=2, replica_groups=mesh['dp'=32,'expert'=16] {'dp'}, use_global_device_ids=true, to_apply=%region_4.5.clone | all-reduce | flops 2048 | bytes 16384
  247.9 0.1 dynamic-slice.2
  248.0 0.7 all_to_all.44
  248.7 7.5 %all-to-all-start.2 = ((f32[16,1,4]{2,1,0:T(1,128)}), f32[16,1,4]{2,1,0:T(1,128)S(1)}, u32[]{:S(2)}, u32[]{:S(2)}) async-start(f32[16,1,4]{2,1,0:T(1,128)} %bitcast.3), calls=%async_computation.2 | async-start | bytes 16384 | tf_op jit(solution)/shard_map/all_to_all | solution.py:55
  256.2 0.1 copy.45
  256.3 0.1 reshape.98
  256.4 7.3 %all-to-all-done.2 = f32[16,1,4]{2,1,0:T(1,128)S(1)} async-done(((f32[16,1,4]{2,1,0:T(1,128)}), f32[16,1,4]{2,1,0:T(1,128)S(1)}, u32[]{:S(2)}, u32[]{:S(2)}) %all-to-all-start.2) | async-done | bytes 288 | tf_op jit(solution)/shard_map/all_to_all | solution.py:55
  263.7 0.5 broadcast.21
  264.2 0.7 reduce.4
  264.9 0.1 broadcast_in_dim.28
  265.0 0.2 select_reduce_fusion
  265.1 0.7 convert_element_type.66
  265.9 3.5 all-to-all-start.3
  270.0 6.8 %all-to-all-done.3 = bf16[16,1,4]{2,1,0:T(2,128)(2,1)S(1)} async-done(((bf16[16,1,4]{2,1,0:T(2,128)(2,1)}), bf16[16,1,4]{2,1,0:T(2,128)(2,1)S(1)}, u32[]{:S(2)}, u32[]{:S(2)}) %all-to-all-start.3) | async-done | bytes 160 | tf_op jit(solution)/shard_map/all_to_all | solution.py:32
  276.8 0.1 reshape.99
  276.9 0.2 dynamic-update-slice
  277.2 71.4 %all-reduce = bf16[2048]{0:T(1024)(128)(2,1)S(1)} all-reduce(bf16[2048]{0:T(1024)(128)(2,1)S(1)} %dynamic-update-slice), channel_id=1, replica_groups=mesh['dp'=32,'expert'=16] {'dp'}, use_global_device_ids=true, to_apply=%add | all-reduce | flops 2048 | bytes 8192
  348.6 1.4 multiply_convert_fusion.4
  350.0 1.3 copy.47
  351.4 11.3 %all-to-all-start.4 = ((bf16[32,64,168]{2,1,0:T(8,128)(2,1)}), bf16[32,64,168]{2,1,0:T(8,128)(2,1)S(1)}, u32[]{:S(2)}, u32[]{:S(2)}) async-start(bf16[32,64,168]{2,1,0:T(8,128)(2,1)} %bitcast.24), calls=%async_computation.4 | async-start | bytes 2097152 | tf_op jit(solution)/shard_map/all_to_all | solution.py:53
  362.6 0.1 reshape.94
  362.7 0.7 copy.49
  363.4 8.5 %fusion.2 = f32[1,168,3072]{2,1,0:T(8,128)} fusion(bf16[2048,168]{1,0:T(8,128)(2,1)S(1)} %bitcast.22, bf16[2048,3072]{1,0:T(8,128)(2,1)} %all-gather.2.cloned.1.call-done, f32[2048]{0:T(1024)S(1)} %convert_element_type.61), kind=kOutput, calls=%fused_computation.3 | convolution fusion | flops 2132803584 | bytes 15343616 | tf_op jit(solution)/shard_map/dot_general | solution.py:50
  371.9 9.0 %all-to-all-done.4 = bf16[32,64,168]{2,1,0:T(8,128)(2,1)S(1)} async-done(((bf16[32,64,168]{2,1,0:T(8,128)(2,1)}), bf16[32,64,168]{2,1,0:T(8,128)(2,1)S(1)}, u32[]{:S(2)}, u32[]{:S(2)}) %all-to-all-start.4) | async-done | bytes 688160 | tf_op jit(solution)/shard_map/all_to_all | solution.py:53
  380.9 0.6 copy.48
  381.5 3.2 reshape.96
  (9 shorter events, 0.1 us)
Async XLA Ops:
  7.2 161.7 %copy-start = (bf16[1,168,3072]{2,1,0:T(8,128)(2,1)S(1)}, bf16[1,168,3072]{2,1,0:T(8,128)(2,1)}, u32[]{:S(2)}) copy-start(bf16[1,168,3072]{2,1,0:T(8,128)(2,1)} %param.9) | copy-start | bytes 3096580
  7.2 161.7 %all-gather.2.cloned.1.call-start = ((), (), s32[]{:S(2)}) async-start(), calls=%async_computation.5 | async-start | bytes 12976128 | tf_op jit(solution)/shard_map/all_gather | solution.py:40
  40.5 215.8 %copy-start.1 = (bf16[8,4]{0,1:T(4,128)(2,1)S(1)}, bf16[8,4]{0,1:T(4,128)(2,1)}, u32[]{:S(2)}) copy-start(bf16[8,4]{0,1:T(4,128)(2,1)} %param.7) | copy-start | bytes 196
  40.5 49.8 %all-to-all-start = ((bf16[64,32,168]{2,0,1:T(8,128)(2,1)}), bf16[64,32,168]{2,0,1:T(8,128)(2,1)S(1)}, u32[]{:S(2)}, u32[]{:S(2)}) async-start(bf16[64,32,168]{2,0,1:T(8,128)(2,1)} %copy.40), calls=%async_computation | async-start | bytes 2097152 | tf_op jit(solution)/shard_map/all_to_all | solution.py:37
  248.7 15.0 %all-to-all-start.2 = ((f32[16,1,4]{2,1,0:T(1,128)}), f32[16,1,4]{2,1,0:T(1,128)S(1)}, u32[]{:S(2)}, u32[]{:S(2)}) async-start(f32[16,1,4]{2,1,0:T(1,128)} %bitcast.3), calls=%async_computation.2 | async-start | bytes 16384 | tf_op jit(solution)/shard_map/all_to_all | solution.py:55
  265.9 10.9 %all-to-all-start.3 = ((bf16[16,1,4]{2,1,0:T(2,128)(2,1)}), bf16[16,1,4]{2,1,0:T(2,128)(2,1)S(1)}, u32[]{:S(2)}, u32[]{:S(2)}) async-start(bf16[16,1,4]{2,1,0:T(2,128)(2,1)} %convert_element_type.66), calls=%async_computation.3 | async-start | bytes 16384 | tf_op jit(solution)/shard_map/all_to_all | solution.py:32
  351.4 29.5 %all-to-all-start.4 = ((bf16[32,64,168]{2,1,0:T(8,128)(2,1)}), bf16[32,64,168]{2,1,0:T(8,128)(2,1)S(1)}, u32[]{:S(2)}, u32[]{:S(2)}) async-start(bf16[32,64,168]{2,1,0:T(8,128)(2,1)} %bitcast.24), calls=%async_computation.4 | async-start | bytes 2097152 | tf_op jit(solution)/shard_map/all_to_all | solution.py:53
Sparse Core Ops, SparseCore 0:
  34.9 133.9 all-gather.1
where the time goes:
time: 392 us
  blocking collectives  164 us (42%)
  waiting for transfers between devices  139 us (35%)
  starting transfers between devices  32.6 us (8%)
  matrix products  19.6 us (5%)
  local copies, waits for them, and re-layouts  18.1 us (5%)
  between operations  15.4 us (4%)
    unnamed x2, blocking collectives  140 us
    all_gather x1, waiting for transfers between devices, body(): lax.all_gather(dy_rows, 'dp', axis=0, tiled=True)  78.1 us
    all_to_all x1, waiting for transfers between devices, body(): lax.all_to_all(h_rows, 'dp', split_axis=1, concat_axis=0, tiled=True)  37.5 us
    all_to_all x1, blocking collectives, body(): lax.all_to_all(dy_buf.reshape(nexp, cap, width), 'expert', split_axis=0,...  23.9 us
    all_to_all x1, starting transfers between devices, body(): lax.all_to_all(dh_cols, 'dp', split_axis=0, concat_axis=1, tiled=True)  11.3 us
    all_to_all x1, starting transfers between devices, body(): lax.all_to_all(h_rows, 'dp', split_axis=1, concat_axis=0, tiled=True)  10.3 us
    dot_general x1, matrix products, body(): lax.dot_general(dy_all, w_local, (((1,), (1,)), ((), ())), preferred_elem...  9.96 us
    all_to_all x1, waiting for transfers between devices, body(): lax.all_to_all(dh_cols, 'dp', split_axis=0, concat_axis=1, tiled=True)  8.96 us
  transfers between devices with their start and end apart: 5, of which 5 were waited for; matrix products, arithmetic and copies ran while one was open for 3% of the time, Pallas kernels for 0%

commit v1 on v0

v1 whole, which is shorter than its diff:
```python
import jax
import jax.numpy as jnp
from jax import lax
from jax.sharding import Mesh, PartitionSpec as P

YS, XS = 8, 4
F32, BF16 = jnp.float32, jnp.bfloat16


def shift(a, step):
    return lax.ppermute(a, "x", [(i, (i + step) % XS) for i in range(XS)])


def gather_w(w, x):
    n = w.shape[0]
    half = n // 16 * 8
    left, right = shift(w, 1), shift(w, -1)
    far_a, far_b = shift(left[:half], 1), shift(right[half:], -1)
    out = jnp.zeros((XS * n, w.shape[1]), w.dtype)
    put = lambda o, v, at: lax.dynamic_update_slice(o, v, (at, 0))
    out = put(out, w, x * n)
    out = put(out, left, (x + XS - 1) % XS * n)
    out = put(out, right, (x + 1) % XS * n)
    out = put(out, far_a, (x + 2) % XS * n)
    return put(out, far_b, (x + 2) % XS * n + half)


def body(grad_out, routes, probs, hidden, w_down):
    tok, width = grad_out.shape
    topk = routes.shape[1]
    cap, feat = hidden.shape[3], hidden.shape[4]
    nexp = lax.axis_size("expert")
    rows = nexp * cap
    share = w_down.shape[1]
    cols = XS * share
    x = lax.axis_index("x")

    w = w_down.reshape(share, width)
    w_cols = gather_w(w, x)

    flat = routes.reshape(-1)
    onehot = (flat[:, None] == jnp.arange(nexp, dtype=jnp.int32)[None, :]).astype(jnp.int32)
    before = jnp.cumsum(onehot, axis=0) - onehot
    slot = jnp.sum(before * onehot, axis=1)
    target = flat * cap + slot
    select = target[:, None] == jnp.arange(rows, dtype=jnp.int32)[None, :]
    sel_tok = jnp.sum(select.reshape(tok, topk, rows).astype(F32), axis=1).astype(BF16)
    dy_buf = jnp.dot(sel_tok.T, grad_out, preferred_element_type=F32).astype(BF16)
    p_buf = jnp.sum(jnp.where(select, probs.reshape(-1)[:, None].astype(F32), 0.0), axis=0)
    p_pad = jnp.broadcast_to(p_buf.astype(BF16)[:, None], (rows, 128))
    send = jnp.concatenate([dy_buf, p_pad], axis=1).reshape(nexp, cap, width + 128)
    recv = lax.all_to_all(send, "expert", split_axis=0, concat_axis=0, tiled=True)
    recv = recv.reshape(rows, width + 128)
    every = lax.all_gather(recv, "y", axis=0, tiled=True)

    h = hidden.reshape(rows, YS, cols).transpose(1, 0, 2)
    h, _ = lax.optimization_barrier((h, recv[:1, :1]))
    h = lax.all_to_all(h, "y", split_axis=0, concat_axis=0, tiled=True).reshape(YS * rows, cols)
    h_t = h.T

    dy = every[:, :width]
    p = every[:, width : width + 1].astype(F32)
    g = (p * dy.astype(F32)).astype(BF16)
    h_t, g = lax.optimization_barrier((h_t, g))

    def part(step):
        block = lax.dynamic_slice(h_t, ((x + step) % XS * share, 0), (share, YS * rows))
        return jnp.dot(block, g, preferred_element_type=F32)

    half = share // 16 * 8
    far = part(2).astype(BF16)
    from_a, from_b = shift(far[:half], 1), shift(far[half:], -1)
    up, down, own = part(1), part(3), part(0)
    up = jnp.concatenate([up[:half] + from_a.astype(F32), up[half:]], axis=0).astype(BF16)
    down = jnp.concatenate([down[:half], down[half:] + from_b.astype(F32)], axis=0).astype(BF16)
    d_down = own + shift(up, 1).astype(F32) + shift(down, -1).astype(F32)

    u = lax.dot_general(dy, w_cols, (((1,), (1,)), ((), ())), preferred_element_type=F32)
    dh = (p * u).astype(BF16)
    value = jnp.sum(h.astype(F32) * u, axis=1, keepdims=True)
    high = lax.reduce_precision(value, 8, 7)
    back = jnp.concatenate([dh, high.astype(BF16), (value - high).astype(BF16)], axis=1)
    back = lax.all_to_all(
        back.reshape(YS, rows, cols + 2), "y", split_axis=0, concat_axis=0, tiled=True
    )
    d_hidden = back[:, :, :cols].transpose(1, 0, 2).reshape(hidden.shape)
    d_slot = jnp.sum(back[:, :, cols:].astype(F32), axis=(0, 2))
    returned = lax.all_to_all(
        d_slot.reshape(nexp, cap), "expert", split_axis=0, concat_axis=0, tiled=True
    )
    d_probs = jnp.sum(jnp.where(select, returned.reshape(-1)[None, :], 0.0), axis=1)
    return d_probs.reshape(tok, topk), d_hidden, d_down.reshape(w_down.shape)


def solution(mesh):
    grid = Mesh(mesh.devices.reshape(YS, XS, -1), ("y", "x", "expert"))
    tokens = P(("y", "x", "expert"), None)
    saved = P(("y", "x"), "expert", None, None, None)
    weight = P("expert", ("y", "x"), None)
    return jax.shard_map(
        body,
        mesh=grid,
        in_specs=(tokens, tokens, tokens, saved, weight),
        out_specs=(tokens, saved, weight),
        check_vma=False,
    )
```

time: 392 us -> 185 us (0.47)
  blocking collectives: 164 us -> 24.2 us
  waiting for transfers between devices: 139 us -> 40.2 us
  local copies, waits for them, and re-layouts: 18.1 us -> 31.6 us
  other arithmetic: 2.75 us -> 15.5 us
  starting transfers between devices: 32.6 us -> 42.4 us
  matrix products: 19.6 us -> 14.5 us
    unnamed x2 -> x0, blocking collectives: 140 us -> none
    all_gather x1, waiting for transfers between devices: 78.1 us -> 9.54 us  [body(): every = lax.all_gather(recv, 'y', axis=0, tiled=True)]
    all_to_all x3 -> x2, waiting for transfers between devices: 53.2 us -> 12.7 us  [the longest x1 12.7 us: body(): lax.all_to_all(h, 'y', split_axis=0, concat_axis=0, tiled=True)]
    ppermute x0 -> x8, starting transfers between devices: none -> 23.3 us  [shift(): return lax.ppermute(a, 'x', [(i, (i + step) % XS) for i in range(XS)])]
    ppermute x0 -> x8, waiting for transfers between devices: none -> 13.9 us  [shift(): return lax.ppermute(a, 'x', [(i, (i + step) % XS) for i in range(XS)])]
    all_to_all x3 -> x2, starting transfers between devices: 25.1 us -> 11.6 us  [the longest x1 7.11 us: body(): lax.all_to_all(h, 'y', split_axis=0, concat_axis=0, tiled=True)]
    dynamic_update_slice x0 -> x5, local copies, waits for them, and re-layouts: none -> 6.92 us  [gather_w(): put = lambda o, v, at: lax.dynamic_update_slice(o, v, (at, 0))]
    all_to_all x4 -> x0, local copies, waits for them, and re-layouts: 6.77 us -> none  [the longest x3 6.18 us: body(): lax.all_to_all(h_rows, 'dp', split_axis=1, concat_axis=0, tiled=True)]
  transfers between devices with their start and end apart: 5 -> 12, of which waited for: 5 -> 6; matrix products, arithmetic and copies ran while one was open for 3% -> 21% of each run, Pallas kernels for 0% -> 0%
where the time goes in v1:
time: 185 us; the launch traced here: 183 us
  starting transfers between devices  42.4 us (23%)
  waiting for transfers between devices  40.2 us (22%)
  local copies, waits for them, and re-layouts  31.6 us (17%)
  blocking collectives  24.2 us (13%)
  other arithmetic  15.5 us (8%)
  matrix products  14.5 us (8%)
  between operations  14.3 us (8%)
    all_to_all x1, blocking collectives, body(): lax.all_to_all(send, 'expert', split_axis=0, concat_axis=0, tiled=True)  24.2 us
    ppermute x8, starting transfers between devices, shift(): return lax.ppermute(a, 'x', [(i, (i + step) % XS) for i in range(XS)])  23.3 us
    ppermute x8, waiting for transfers between devices, shift(): return lax.ppermute(a, 'x', [(i, (i + step) % XS) for i in range(XS)])  13.9 us
    all_to_all x1, waiting for transfers between devices, body(): lax.all_to_all(h, 'y', split_axis=0, concat_axis=0, tiled=True)  12.7 us
    all_gather x1, waiting for transfers between devices, body(): every = lax.all_gather(recv, 'y', axis=0, tiled=True)  9.54 us
    dot_general x4, matrix products, part(): return jnp.dot(block, g, preferred_element_type=F32)  8.82 us
    all_to_all x1, starting transfers between devices, body(): lax.all_to_all(d_slot.reshape(nexp, cap), 'expert', split_axis=0, concat_...  7.48 us
    all_to_all x1, starting transfers between devices, body(): lax.all_to_all(h, 'y', split_axis=0, concat_axis=0, tiled=True)  7.11 us
  transfers between devices with their start and end apart: 12, of which 6 were waited for; matrix products, arithmetic and copies ran while one was open for 21% of the time, Pallas kernels for 0%

profile of v1, /device:TPU:6, one launch (start us, length us, event | category | flops | bytes accessed | tf_op | source)
XLA Modules:
  0.0 182.7 jit_solution(16434773332841789273)
XLA Ops:
  10.1 24.2 %all_to_all.24 = bf16[16,4,3200]{2,1,0:T(4,128)(2,1)S(1)} all-to-all(bf16[16,4,3200]{2,1,0:T(4,128)(2,1)S(1)} %reshape.110), channel_id=1, replica_groups=mesh['y'=8,'x'=4,'expert'=16] {'expert'}, dimensions={0} | all-to-all | bytes 819200 | tf_op jit(solution)/shard_map/all_to_all | solution.py:52
  34.3 0.9 reshape.111
  35.2 2.4 %collective-permute-start = (bf16[168,3072]{1,0:T(8,128)(2,1)}, bf16[168,3072]{1,0:T(8,128)(2,1)S(1)}, u32[]{:S(2)}, u32[]{:S(2)}) collective-permute-start(bf16[168,3072]{1,0:T(8,128)(2,1)} %bitcast.27), channel_id=1, source_target_pairs={{0,16},{16,32},{32,48},{48,0},{1,17},{17,33},{33,49},{49,1},{2,18}... | collective-permute-start | bytes 3096584 | tf_op jit(solution)/shard_map/ppermute | solution.py:11
  37.6 3.5 %collective-permute-start.1 = (bf16[168,3072]{1,0:T(8,128)(2,1)}, bf16[168,3072]{1,0:T(8,128)(2,1)S(1)}, u32[]{:S(2)}, u32[]{:S(2)}) collective-permute-start(bf16[168,3072]{1,0:T(8,128)(2,1)} %bitcast.28), channel_id=1, source_target_pairs={{0,48},{16,0},{32,16},{48,32},{1,49},{17,1},{33,17},{49,33},{2,50}... | collective-permute-start | bytes 3096584 | tf_op jit(solution)/shard_map/ppermute | solution.py:11
  41.1 2.4 %reshape.113 = bf16[64,8,672]{2,1,0:T(8,128)(2,1)S(1)} reshape(bf16[1,1,16,4,5376]{4,3,2,1,0:T(4,128)(2,1)} %param.8) | data formatting | bytes 1376256 | tf_op jit(solution)/shard_map/reshape | solution.py:56
  43.5 1.0 copy.68
  44.5 7.1 %all-to-all-start.1 = ((bf16[8,64,672]{2,1,0:T(8,128)(2,1)}), bf16[8,64,672]{2,1,0:T(8,128)(2,1)S(1)}, u32[]{:S(2)}, u32[]{:S(2)}) async-start(bf16[8,64,672]{2,1,0:T(8,128)(2,1)} %bitcast.20), calls=%async_computation.1 | async-start | bytes 1572864 | tf_op jit(solution)/shard_map/all_to_all | solution.py:58
  51.6 2.4 %broadcast_in_dim.40 = bf16[672,3072]{1,0:T(8,128)(2,1)} broadcast(bf16[]{:T(256)} %constant.56.clone.1), dimensions={} | broadcast | bytes 4128770 | tf_op jit(solution)/shard_map/broadcast_in_dim | solution.py:19
  54.1 1.0 constant_dynamic-update-slice_fusion.4
  55.1 7.6 %collective-permute-done = bf16[168,3072]{1,0:T(8,128)(2,1)S(1)} collective-permute-done((bf16[168,3072]{1,0:T(8,128)(2,1)}, bf16[168,3072]{1,0:T(8,128)(2,1)S(1)}, u32[]{:S(2)}, u32[]{:S(2)}) %collective-permute-start) | collective-permute-done | bytes 1032224 | tf_op jit(solution)/shard_map/ppermute | solution.py:11
  62.7 0.8 slice.53
  63.6 3.6 %collective-permute-start.2 = (bf16[80,3072]{1,0:T(8,128)(2,1)}, bf16[80,3072]{1,0:T(8,128)(2,1)}, u32[]{:S(2)}, u32[]{:S(2)}) collective-permute-start(bf16[80,3072]{1,0:T(8,128)(2,1)} %slice.53), channel_id=1, source_target_pairs={{0,16},{16,32},{32,48},{48,0},{1,17},{17,33},{33,49},{49,1},{2,18}... | collective-permute-start | bytes 1474568 | tf_op jit(solution)/shard_map/ppermute | solution.py:11
  67.2 2.2 %collective-permute-start.3 = (bf16[88,3072]{1,0:T(8,128)(2,1)S(1)}, bf16[88,3072]{1,0:T(8,128)(2,1)}, u32[]{:S(2)}, u32[]{:S(2)}) collective-permute-start(bf16[88,3072]{1,0:T(8,128)(2,1)S(1)} %slice.54), channel_id=1, source_target_pairs={{0,48},{16,0},{32,16},{48,32},{1,49},{17,1},{33,17},{49,33},{2,50}... | collective-permute-start | bytes 1622024 | tf_op jit(solution)/shard_map/ppermute | solution.py:11
  69.5 1.1 constant_dynamic-update-slice_fusion.3
  70.5 1.1 constant_dynamic-update-slice_fusion.2
  71.6 12.7 %all-to-all-done.1 = bf16[8,64,672]{2,1,0:T(8,128)(2,1)S(1)} async-done(((bf16[8,64,672]{2,1,0:T(8,128)(2,1)}), bf16[8,64,672]{2,1,0:T(8,128)(2,1)S(1)}, u32[]{:S(2)}, u32[]{:S(2)}) %all-to-all-start.1) | async-done | bytes 688160 | tf_op jit(solution)/shard_map/all_to_all | solution.py:58
  84.3 1.1 copy.61
  85.4 1.9 %constant_dynamic-update-slice_fusion.1 = bf16[672,3072]{1,0:T(8,128)(2,1)} fusion(bf16[672,3072]{1,0:T(8,128)(2,1)} %constant_dynamic-update-slice_fusion.2, bf16[80,3072]{1,0:T(8,128)(2,1)} %collective-permute-done.2, s32[]{:T(128)S(6)} %select_n.63), kind=kLoop, calls=%fused_computation.45 | loop fusion | bytes 983044 | tf_op jit(solution)/shard_map/dynamic_update_slice | solution.py:20
  87.2 1.9 %constant_dynamic-update-slice_fusion = bf16[672,3072]{1,0:T(8,128)(2,1)} fusion(bf16[672,3072]{1,0:T(8,128)(2,1)} %constant_dynamic-update-slice_fusion.1, bf16[88,3072]{1,0:T(8,128)(2,1)} %collective-permute-done.3, s32[]{:T(128)S(6)} %select_n.64), kind=kLoop, calls=%fused_computation.44 | loop fusion | bytes 1081348 | tf_op jit(solution)/shard_map/dynamic_update_slice | solution.py:20
  89.1 9.5 %all-gather.2.cloned.1.call-done = bf16[512,3200]{1,0:T(8,128)(2,1)} async-done(((bf16[64,3200]{1,0:T(8,128)(2,1)}), bf16[512,3200]{1,0:T(8,128)(2,1)}) %all-gather.2.cloned.1.call-update) | async-done | bytes 3276816 | tf_op jit(solution)/shard_map/all_gather | solution.py:54
  98.7 1.0 convert_reduce_fusion
  99.7 2.9 %multiply_convert_fusion = bf16[512,3072]{1,0:T(8,128)(2,1)S(1)} fusion(f32[512]{0:T(512)S(1)} %convert_reduce_fusion, bf16[512,3200]{1,0:T(8,128)(2,1)} %all-gather.2.cloned.1.call-done), kind=kLoop, calls=%fused_computation | loop fusion | flops 4718592 | bytes 6293504 | tf_op jit(solution)/shard_map/convert_element_type | solution.py:63
  102.7 2.1 %fusion.4 = f32[168,3072]{1,0:T(8,128)} fusion(bf16[512,3072]{1,0:T(8,128)(2,1)S(1)} %multiply_convert_fusion, bf16[672,512]{0,1:T(8,128)(2,1)S(1)} %bitcast.24, s32[]{:T(128)S(6)} %select_n.59), kind=kOutput, calls=%fused_computation.21 | convolution fusion | flops 528482304 | bytes 5472260 | tf_op jit(solution)/shard_map/dot_general | solution.py:68
  104.8 1.8 convolution_convert_fusion
  107.2 5.4 %multiply_convert_fusion.1 = (bf16[512,672]{0,1:T(8,128)(2,1)}, f32[512]{0:T(512)S(1)}) fusion(f32[512]{0:T(512)S(1)} %convert_reduce_fusion, bf16[512,672]{0,1:T(8,128)(2,1)S(1)} %copy-done.7, bf16[672,3072]{1,0:T(8,128)(2,1)} %constant_dynamic-update-slice_fusion, bf16[512,3200]{1,0:T(8,128)(2,1)S(1)} %copy-done.5), kind=kOutput, calls=%fused_computation.7 | convolution fusion | flops 2115649024 | bytes 8654848 | tf_op jit(solution)/shard_map/dot_general | solution.py:78
  112.7 1.8 %slice.58 = bf16[80,3072]{1,0:T(8,128)(2,1)} slice(bf16[168,3072]{1,0:T(8,128)(2,1)} %convolution_convert_fusion), slice={[0:80], [0:3072]} | slice | bytes 983040 | tf_op jit(solution)/shard_map/slice | solution.py:72
  114.6 2.4 %collective-permute-start.4 = (bf16[80,3072]{1,0:T(8,128)(2,1)}, bf16[80,3072]{1,0:T(8,128)(2,1)}, u32[]{:S(2)}, u32[]{:S(2)}) collective-permute-start(bf16[80,3072]{1,0:T(8,128)(2,1)} %slice.58), channel_id=1, source_target_pairs={{0,16},{16,32},{32,48},{48,0},{1,17},{17,33},{33,49},{49,1},{2,18}... | collective-permute-start | bytes 1474568 | tf_op jit(solution)/shard_map/ppermute | solution.py:11
  117.0 1.9 %slice.62 = bf16[88,3072]{1,0:T(8,128)(2,1)} slice(bf16[168,3072]{1,0:T(8,128)(2,1)} %convolution_convert_fusion), slice={[80:168], [0:3072]} | slice | bytes 1081344 | tf_op jit(solution)/shard_map/slice | solution.py:72
  119.2 2.3 %copy.59 = bf16[512,672]{1,0:T(8,128)(2,1)} copy(bf16[512,672]{0,1:T(8,128)(2,1)} %get-tuple-element.25) | data formatting | bytes 1376256 | tf_op jit(solution)/shard_map/convert_element_type | solution.py:79
  121.5 2.2 %pad_maximum_fusion.2 = bf16[8,64,674]{2,1,0:T(8,128)(2,1)} fusion(bf16[8,64,1]{2,1,0:T(8,128)(2,1)S(1)} %copy.63, bf16[8,64,1]{2,1,0:T(8,128)(2,1)S(1)} %copy.62, bf16[8,64,672]{2,1,0:T(8,128)(2,1)} %bitcast.26), kind=kLoop, calls=%fused_computation.17 | loop fusion | flops 2070528 | bytes 1380352 | tf_op jit(solution)/shard_map/concatenate | solution.py:82
  123.7 4.5 %all-to-all-start.2 = ((bf16[8,64,674]{2,1,0:T(8,128)(2,1)}), bf16[8,64,674]{2,1,0:T(8,128)(2,1)}, u32[]{:S(2)}, u32[]{:S(2)}) async-start(bf16[8,64,674]{2,1,0:T(8,128)(2,1)} %pad_maximum_fusion.2), calls=%async_computation.2 | async-start | bytes 1572864 | tf_op jit(solution)/shard_map/all_to_all | solution.py:83
  128.2 3.4 %collective-permute-start.6 = (bf16[88,3072]{1,0:T(8,128)(2,1)}, bf16[88,3072]{1,0:T(8,128)(2,1)S(1)}, u32[]{:S(2)}, u32[]{:S(2)}) collective-permute-start(bf16[88,3072]{1,0:T(8,128)(2,1)} %slice.62), channel_id=1, source_target_pairs={{0,48},{16,0},{32,16},{48,32},{1,49},{17,1},{33,17},{49,33},{2,50}... | collective-permute-start | bytes 1622024 | tf_op jit(solution)/shard_map/ppermute | solution.py:11
  131.6 1.3 slice.78
  132.8 1.8 fusion.7
  134.7 1.3 fusion.3
  136.0 1.1 pad_maximum_fusion
  137.1 3.7 %collective-permute-start.5 = (bf16[168,3072]{1,0:T(8,128)(2,1)}, bf16[168,3072]{1,0:T(8,128)(2,1)}, u32[]{:S(2)}, u32[]{:S(2)}) collective-permute-start(bf16[168,3072]{1,0:T(8,128)(2,1)} %pad_maximum_fusion), channel_id=1, source_target_pairs={{0,16},{16,32},{32,48},{48,0},{1,17},{17,33},{33,49},{49,1},{2,18}... | collective-permute-start | bytes 3096584 | tf_op jit(solution)/shard_map/ppermute | solution.py:11
  140.8 4.2 %collective-permute-done.6 = bf16[88,3072]{1,0:T(8,128)(2,1)S(1)} collective-permute-done((bf16[88,3072]{1,0:T(8,128)(2,1)}, bf16[88,3072]{1,0:T(8,128)(2,1)S(1)}, u32[]{:S(2)}, u32[]{:S(2)}) %collective-permute-start.6) | collective-permute-done | bytes 540704 | tf_op jit(solution)/shard_map/ppermute | solution.py:11
  145.0 1.0 pad_maximum_fusion.1
  146.1 2.2 %collective-permute-start.7 = (bf16[168,3072]{1,0:T(8,128)(2,1)}, bf16[168,3072]{1,0:T(8,128)(2,1)}, u32[]{:S(2)}, u32[]{:S(2)}) collective-permute-start(bf16[168,3072]{1,0:T(8,128)(2,1)} %pad_maximum_fusion.1), channel_id=1, source_target_pairs={{0,48},{16,0},{32,16},{48,32},{1,49},{17,1},{33,17},{49,33},{2,50}... | collective-permute-start | bytes 3096584 | tf_op jit(solution)/shard_map/ppermute | solution.py:11
  148.3 3.1 %fusion.9 = f32[168,3072]{1,0:T(8,128)} fusion(bf16[512,3072]{1,0:T(8,128)(2,1)S(1)} %multiply_convert_fusion, bf16[672,512]{0,1:T(8,128)(2,1)} %bitcast.23, s32[]{:T(128)S(6)} %select_n.67), kind=kOutput, calls=%fused_computation.26 | convolution fusion | flops 528482304 | bytes 5472260 | tf_op jit(solution)/shard_map/dot_general | solution.py:68
  151.4 1.3 convert_reduce_fusion.1
  153.4 7.5 %all-to-all-start.3 = ((f32[16,1,4]{2,1,0:T(1,128)}), f32[16,1,4]{2,1,0:T(1,128)S(1)}, u32[]{:S(2)}, u32[]{:S(2)}) async-start(f32[16,1,4]{2,1,0:T(1,128)} %bitcast.4), calls=%async_computation.3 | async-start | bytes 16384 | tf_op jit(solution)/shard_map/all_to_all | solution.py:88
  160.8 1.2 slice_bitcast_fusion
  162.5 1.8 %reshape.116 = bf16[1,1,16,4,5376]{4,3,2,1,0:T(4,128)(2,1)} reshape(bf16[64,8,672]{2,1,0:T(8,128)(2,1)S(1)} %copy.65) | data formatting | bytes 1376256 | tf_op jit(solution)/shard_map/reshape | solution.py:86
  164.3 4.1 %all-to-all-done.3 = f32[16,1,4]{2,1,0:T(1,128)S(1)} async-done(((f32[16,1,4]{2,1,0:T(1,128)}), f32[16,1,4]{2,1,0:T(1,128)S(1)}, u32[]{:S(2)}, u32[]{:S(2)}) %all-to-all-start.3) | async-done | bytes 288 | tf_op jit(solution)/shard_map/all_to_all | solution.py:88
  170.6 2.1 %collective-permute-done.7 = bf16[168,3072]{1,0:T(8,128)(2,1)} collective-permute-done((bf16[168,3072]{1,0:T(8,128)(2,1)}, bf16[168,3072]{1,0:T(8,128)(2,1)}, u32[]{:S(2)}, u32[]{:S(2)}) %collective-permute-start.7) | collective-permute-done | bytes 1032224 | tf_op jit(solution)/shard_map/ppermute | solution.py:11
  172.7 3.2 %add_bitcast_fusion = f32[1,168,3072]{2,1,0:T(8,128)} fusion(bf16[168,3072]{1,0:T(8,128)(2,1)} %collective-permute-done.7, f32[168,3072]{1,0:T(8,128)S(1)} %copy-done.3, bf16[168,3072]{1,0:T(8,128)(2,1)} %collective-permute-done.5), kind=kLoop, calls=%fused_computation.5 | loop fusion | flops 2064384 | bytes 6193152 | tf_op jit(solution)/shard_map/reshape | solution.py:92
  (56 shorter events, 7.5 us)
Async XLA Ops:
  7.2 2.4 %copy-start = (bf16[8,3072]{1,0:T(8,128)(2,1)S(1)}, bf16[8,3072]{1,0:T(8,128)(2,1)}, u32[]{:S(2)}) copy-start(bf16[8,3072]{1,0:T(8,128)(2,1)} %param.5) | copy-start | bytes 147460
  7.2 91.5 %all-gather.2.cloned.1.call-start = ((), (), s32[]{:S(2)}) async-start(), calls=%async_computation.4 | async-start | bytes 3686400 | tf_op jit(solution)/shard_map/all_gather | solution.py:54
  35.2 27.5 %collective-permute-start = (bf16[168,3072]{1,0:T(8,128)(2,1)}, bf16[168,3072]{1,0:T(8,128)(2,1)S(1)}, u32[]{:S(2)}, u32[]{:S(2)}) collective-permute-start(bf16[168,3072]{1,0:T(8,128)(2,1)} %bitcast.27), channel_id=1, source_target_pairs={{0,16},{16,32},{32,48},{48,0},{1,17},{17,33},{33,49},{49,1},{2,18}... | collective-permute-start | bytes 3096584 | tf_op jit(solution)/shard_map/ppermute | solution.py:11
  37.6 29.6 %collective-permute-start.1 = (bf16[168,3072]{1,0:T(8,128)(2,1)}, bf16[168,3072]{1,0:T(8,128)(2,1)S(1)}, u32[]{:S(2)}, u32[]{:S(2)}) collective-permute-start(bf16[168,3072]{1,0:T(8,128)(2,1)} %bitcast.28), channel_id=1, source_target_pairs={{0,48},{16,0},{32,16},{48,32},{1,49},{17,1},{33,17},{49,33},{2,50}... | collective-permute-start | bytes 3096584 | tf_op jit(solution)/shard_map/ppermute | solution.py:11
  44.5 39.7 %all-to-all-start.1 = ((bf16[8,64,672]{2,1,0:T(8,128)(2,1)}), bf16[8,64,672]{2,1,0:T(8,128)(2,1)S(1)}, u32[]{:S(2)}, u32[]{:S(2)}) async-start(bf16[8,64,672]{2,1,0:T(8,128)(2,1)} %bitcast.20), calls=%async_computation.1 | async-start | bytes 1572864 | tf_op jit(solution)/shard_map/all_to_all | solution.py:58
  51.6 2.4 %copy-start.6 = (bf16[1,168,3072]{2,1,0:T(8,128)(2,1)S(1)}, bf16[1,168,3072]{2,1,0:T(8,128)(2,1)}, u32[]{:S(2)}) copy-start(bf16[1,168,3072]{2,1,0:T(8,128)(2,1)} %param.9) | copy-start | bytes 3096580
  63.6 21.8 %collective-permute-start.2 = (bf16[80,3072]{1,0:T(8,128)(2,1)}, bf16[80,3072]{1,0:T(8,128)(2,1)}, u32[]{:S(2)}, u32[]{:S(2)}) collective-permute-start(bf16[80,3072]{1,0:T(8,128)(2,1)} %slice.53), channel_id=1, source_target_pairs={{0,16},{16,32},{32,48},{48,0},{1,17},{17,33},{33,49},{49,1},{2,18}... | collective-permute-start | bytes 1474568 | tf_op jit(solution)/shard_map/ppermute | solution.py:11
  67.2 20.0 %collective-permute-start.3 = (bf16[88,3072]{1,0:T(8,128)(2,1)S(1)}, bf16[88,3072]{1,0:T(8,128)(2,1)}, u32[]{:S(2)}, u32[]{:S(2)}) collective-permute-start(bf16[88,3072]{1,0:T(8,128)(2,1)S(1)} %slice.54), channel_id=1, source_target_pairs={{0,48},{16,0},{32,16},{48,32},{1,49},{17,1},{33,17},{49,33},{2,50}... | collective-permute-start | bytes 1622024 | tf_op jit(solution)/shard_map/ppermute | solution.py:11
  84.3 14.4 %copy-start.1 = (bf16[8,64,672]{2,1,0:T(8,128)(2,1)}, bf16[8,64,672]{2,1,0:T(8,128)(2,1)S(1)}, u32[]{:S(2)}) copy-start(bf16[8,64,672]{2,1,0:T(8,128)(2,1)S(1)} %all-to-all-done.1) | copy-start | bytes 2064388
  99.7 3.0 %copy-start.2 = (bf16[8,64,672]{2,1,0:T(8,128)(2,1)S(1)}, bf16[8,64,672]{2,1,0:T(8,128)(2,1)}, u32[]{:S(2)}) copy-start(bf16[8,64,672]{2,1,0:T(8,128)(2,1)} %copy-done.1) | copy-start | bytes 2064388
  104.8 2.3 %copy-start.5 = (bf16[512,3200]{1,0:T(8,128)(2,1)S(1)}, bf16[512,3200]{1,0:T(8,128)(2,1)}, u32[]{:S(2)}) copy-start(bf16[512,3200]{1,0:T(8,128)(2,1)} %all-gather.2.cloned.1.call-done) | copy-start | bytes 9830404
  104.8 2.5 %copy-start.7 = (bf16[512,672]{0,1:T(8,128)(2,1)S(1)}, bf16[512,672]{0,1:T(8,128)(2,1)}, u32[]{:S(2)}) copy-start(bf16[512,672]{0,1:T(8,128)(2,1)} %copy.61) | copy-start | bytes 2064388
  114.6 20.2 %collective-permute-start.4 = (bf16[80,3072]{1,0:T(8,128)(2,1)}, bf16[80,3072]{1,0:T(8,128)(2,1)}, u32[]{:S(2)}, u32[]{:S(2)}) collective-permute-start(bf16[80,3072]{1,0:T(8,128)(2,1)} %slice.58), channel_id=1, source_target_pairs={{0,16},{16,32},{32,48},{48,0},{1,17},{17,33},{33,49},{49,1},{2,18}... | collective-permute-start | bytes 1474568 | tf_op jit(solution)/shard_map/ppermute | solution.py:11
  123.7 27.7 %all-to-all-start.2 = ((bf16[8,64,674]{2,1,0:T(8,128)(2,1)}), bf16[8,64,674]{2,1,0:T(8,128)(2,1)}, u32[]{:S(2)}, u32[]{:S(2)}) async-start(bf16[8,64,674]{2,1,0:T(8,128)(2,1)} %pad_maximum_fusion.2), calls=%async_computation.2 | async-start | bytes 1572864 | tf_op jit(solution)/shard_map/all_to_all | solution.py:83
  128.2 16.8 %collective-permute-start.6 = (bf16[88,3072]{1,0:T(8,128)(2,1)}, bf16[88,3072]{1,0:T(8,128)(2,1)S(1)}, u32[]{:S(2)}, u32[]{:S(2)}) collective-permute-start(bf16[88,3072]{1,0:T(8,128)(2,1)} %slice.62), channel_id=1, source_target_pairs={{0,48},{16,0},{32,16},{48,32},{1,49},{17,1},{33,17},{49,33},{2,50}... | collective-permute-start | bytes 1622024 | tf_op jit(solution)/shard_map/ppermute | solution.py:11
  134.6 10.3 %copy-start.4 = (f32[168,3072]{1,0:T(8,128)S(1)}, f32[168,3072]{1,0:T(8,128)}, u32[]{:S(2)}) copy-start(f32[168,3072]{1,0:T(8,128)} %fusion.4) | copy-start | bytes 6193156
  137.1 33.5 %collective-permute-start.5 = (bf16[168,3072]{1,0:T(8,128)(2,1)}, bf16[168,3072]{1,0:T(8,128)(2,1)}, u32[]{:S(2)}, u32[]{:S(2)}) collective-permute-start(bf16[168,3072]{1,0:T(8,128)(2,1)} %pad_maximum_fusion), channel_id=1, source_target_pairs={{0,16},{16,32},{32,48},{48,0},{1,17},{17,33},{33,49},{49,1},{2,18}... | collective-permute-start | bytes 3096584 | tf_op jit(solution)/shard_map/ppermute | solution.py:11
  146.1 26.6 %collective-permute-start.7 = (bf16[168,3072]{1,0:T(8,128)(2,1)}, bf16[168,3072]{1,0:T(8,128)(2,1)}, u32[]{:S(2)}, u32[]{:S(2)}) collective-permute-start(bf16[168,3072]{1,0:T(8,128)(2,1)} %pad_maximum_fusion.1), channel_id=1, source_target_pairs={{0,48},{16,0},{32,16},{48,32},{1,49},{17,1},{33,17},{49,33},{2,50}... | collective-permute-start | bytes 3096584 | tf_op jit(solution)/shard_map/ppermute | solution.py:11
  151.4 21.3 %copy-start.3 = (f32[168,3072]{1,0:T(8,128)S(1)}, f32[168,3072]{1,0:T(8,128)}, u32[]{:S(2)}) copy-start(f32[168,3072]{1,0:T(8,128)} %fusion.9) | copy-start | bytes 6193156
  153.4 15.0 %all-to-all-start.3 = ((f32[16,1,4]{2,1,0:T(1,128)}), f32[16,1,4]{2,1,0:T(1,128)S(1)}, u32[]{:S(2)}, u32[]{:S(2)}) async-start(f32[16,1,4]{2,1,0:T(1,128)} %bitcast.4), calls=%async_computation.3 | async-start | bytes 16384 | tf_op jit(solution)/shard_map/all_to_all | solution.py:88
Sparse Core Ops, SparseCore 0:
  35.3 63.3 all-gather.1

commit v2 on v1

v2 whole, which is shorter than its diff:
```python
import jax
import jax.numpy as jnp
from jax import lax
from jax.experimental import pallas as pl
from jax.experimental.pallas import tpu as pltpu
from jax.sharding import Mesh, PartitionSpec as P

YS, XS = 8, 4
F32, BF16 = jnp.float32, jnp.bfloat16
LANES = 128
TILE = 1536


def params(mib=60):
    return pltpu.CompilerParams(vmem_limit_bytes=mib * 1024 * 1024)


def shift(a, step):
    return lax.ppermute(a, "x", [(i, (i + step) % XS) for i in range(XS)])


def gather_w(w, x):
    n = w.shape[0]
    half = n // 32 * 16
    left, right = shift(w, 1), shift(w, -1)
    far_top, far_bottom = shift(left[:half], 1), shift(right[half:], -1)
    out = jnp.zeros((XS * n, w.shape[1]), w.dtype)
    put = lambda o, v, step, low: lax.dynamic_update_slice(o, v, ((x + step) % XS * n + low, 0))
    out = put(put(put(out, w, 0, 0), left, XS - 1, 0), right, 1, 0)
    return put(put(out, far_top, 2, 0), far_bottom, 2, half)


def pack(grad_out, routes, probs, me):
    tok, width = grad_out.shape
    topk = routes.shape[1]

    def kernel(me_ref, dy_ref, r_ref, p_ref, out_ref):
        out_ref[:, :width] = dy_ref[...]
        info = jnp.concatenate([r_ref[...].astype(F32), p_ref[...].astype(F32)], axis=0)
        info = jnp.concatenate([info] * (LANES // tok), axis=1)
        lane = lax.broadcasted_iota(jnp.int32, info.shape, 1)
        out_ref[:, width:] = jnp.where(lane // tok == me_ref[0], info, 0.0).astype(BF16)

    vmem = pl.BlockSpec(memory_space=pltpu.VMEM)
    return pl.pallas_call(
        kernel,
        out_shape=jax.ShapeDtypeStruct((tok, width + LANES), BF16),
        in_specs=[pl.BlockSpec(memory_space=pltpu.SMEM), vmem, vmem, vmem],
        out_specs=vmem,
        compiler_params=params(16),
        cost_estimate=pl.CostEstimate(flops=0, bytes_accessed=100000, transcendentals=0),
        name="pack_tokens",
    )(me, grad_out, routes.T, probs.T)


def pick_kernel(width, topk, tok, cap, me_ref, all_ref, _, out_ref):
    tokens = all_ref.shape[0]
    rows = out_ref.shape[0]
    me = me_ref[0].astype(F32)
    info = all_ref[:, width:].astype(F32)
    info = sum(info[at : at + tok] for at in range(0, tokens, tok))
    chosen = jnp.zeros((1, tokens), F32)
    weight = jnp.zeros((1, tokens), F32)
    for k in range(topk):
        hit = (info[k : k + 1] == me).astype(F32)
        chosen = chosen + hit
        weight = weight + hit * info[topk + k : topk + k + 1]
    older = lax.broadcasted_iota(jnp.int32, (tokens, tokens), 0)
    newer = lax.broadcasted_iota(jnp.int32, (tokens, tokens), 1)
    counts = ((older < newer) & (older // tok == newer // tok)).astype(BF16)
    many = jnp.broadcast_to(chosen, (16, tokens)).astype(BF16)
    before = jnp.dot(many, counts, preferred_element_type=F32)[:1]
    block = lax.broadcasted_iota(jnp.int32, (1, tokens), 1) // tok
    target = jnp.where(chosen > 0, block * cap + before.astype(jnp.int32), -1)
    select = lax.broadcasted_iota(jnp.int32, (rows, tokens), 0) == target
    p = jnp.sum(jnp.where(select, weight, 0.0), axis=1, keepdims=True)
    dy = jnp.dot(select.astype(F32).astype(BF16), all_ref[:, :width], preferred_element_type=F32)
    out_ref[:, :width] = dy.astype(BF16)
    out_ref[:, width:] = jnp.broadcast_to(p, (rows, LANES)).astype(BF16)


def pick(gathered, after, me, width, topk, tok, cap, rows):
    def kernel(*refs):
        pick_kernel(width, topk, tok, cap, *refs)

    return pl.pallas_call(
        kernel,
        out_shape=jax.ShapeDtypeStruct((rows, width + LANES), BF16),
        in_specs=[
            pl.BlockSpec(memory_space=pltpu.SMEM),
            pl.BlockSpec(memory_space=pltpu.VMEM),
            pl.BlockSpec(memory_space=pl.ANY),
        ],
        out_specs=pl.BlockSpec(memory_space=pltpu.VMEM),
        compiler_params=params(16),
        cost_estimate=pl.CostEstimate(
            flops=2 * rows * gathered.shape[0] * width, bytes_accessed=1300000, transcendentals=0
        ),
        name="pick_slots",
    )(me, gathered, after)


def down_parts(every, h_others, h_own, after, width):
    rows = every.shape[0]
    cols, share = h_others.shape[0], h_own.shape[0]

    def kernel(dy_ref, p_ref, others_ref, mine_ref, _, out_ref, own_ref):
        g = (p_ref[:, :1].astype(F32) * dy_ref[...].astype(F32)).astype(BF16)
        out_ref[...] = jnp.dot(others_ref[...], g, preferred_element_type=F32).astype(BF16)
        own_ref[...] = jnp.dot(mine_ref[...], g, preferred_element_type=F32)

    tile = lambda n: pl.BlockSpec((n, TILE), lambda i: (0, i))
    return pl.pallas_call(
        kernel,
        grid=(width // TILE,),
        out_shape=(
            jax.ShapeDtypeStruct((cols, width), BF16),
            jax.ShapeDtypeStruct((share, width), F32),
        ),
        in_specs=[
            tile(rows),
            pl.BlockSpec((rows, LANES), lambda i: (0, width // LANES)),
            pl.BlockSpec((cols, rows), lambda i: (0, 0)),
            pl.BlockSpec((share, rows), lambda i: (0, 0)),
            pl.BlockSpec(memory_space=pl.ANY),
        ],
        out_specs=(tile(cols), tile(share)),
        compiler_params=params(),
        cost_estimate=pl.CostEstimate(
            flops=2 * rows * cols * width, bytes_accessed=12000000, transcendentals=0
        ),
        name="down_parts",
    )(every, every, h_others, h_own, after)


def hidden_parts(every, w_cols, h, width, wide):
    rows = every.shape[0]
    cols = h.shape[1]
    steps = width // TILE
    edge = cols // LANES * LANES

    def kernel(dy_ref, p_ref, w_ref, h_ref, out_ref, acc):
        step = pl.program_id(0)
        term = lax.dot_general(
            dy_ref[...], w_ref[...], (((1,), (1,)), ((), ())), preferred_element_type=F32
        )

        @pl.when(step == 0)
        def _():
            acc[:, :cols] = term

        @pl.when(step > 0)
        def _():
            acc[:, :cols] += term

        @pl.when(step == steps - 1)
        def _():
            p = p_ref[:, :1].astype(F32)
            value = jnp.sum(h_ref[...].astype(F32) * acc[:, :cols], axis=1, keepdims=True)
            high = value.astype(BF16).astype(F32)
            lane = lax.broadcasted_iota(jnp.int32, (rows, wide - edge), 1) + edge
            tail = jnp.where(lane < cols, p * acc[:, edge:], 0.0)
            tail = jnp.where(lane == cols, high, jnp.where(lane == cols + 1, value - high, tail))
            out_ref[:, :edge] = (p * acc[:, :edge]).astype(BF16)
            out_ref[:, edge:] = tail.astype(BF16)

    return pl.pallas_call(
        kernel,
        grid=(steps,),
        out_shape=jax.ShapeDtypeStruct((rows, wide), BF16),
        in_specs=[
            pl.BlockSpec((rows, TILE), lambda i: (0, i)),
            pl.BlockSpec((rows, LANES), lambda i: (0, width // LANES)),
            pl.BlockSpec((cols, TILE), lambda i: (0, i)),
            pl.BlockSpec((rows, cols), lambda i: (0, 0)),
        ],
        out_specs=pl.BlockSpec((rows, wide), lambda i: (0, 0)),
        scratch_shapes=[pltpu.VMEM((rows, wide), F32)],
        compiler_params=params(),
        cost_estimate=pl.CostEstimate(
            flops=2 * rows * cols * width, bytes_accessed=9000000, transcendentals=0
        ),
        name="hidden_parts",
    )(every, every, w_cols, h)


def body(grad_out, routes, probs, hidden, w_down):
    tok, width = grad_out.shape
    topk = routes.shape[1]
    cap, feat = hidden.shape[3], hidden.shape[4]
    nexp = lax.axis_size("expert")
    rows = nexp * cap
    share = w_down.shape[1]
    cols = XS * share
    wide = -(-(cols + 2) // LANES) * LANES
    x = lax.axis_index("x")
    me = lax.axis_index("expert")

    h = hidden.reshape(nexp, cap, YS, cols).transpose(2, 0, 1, 3)
    h = lax.all_to_all(h, "y", split_axis=0, concat_axis=0, tiled=True)

    packed = lax.all_gather(pack(grad_out, routes, probs, me.reshape(1)), "expert", axis=0, tiled=True)
    mine = pick(packed, h, me.reshape(1), width, topk, tok, cap, rows)
    every = lax.all_gather(mine, "y", axis=0, tiled=True)

    w_cols = gather_w(w_down.reshape(share, width), x)
    h = h.reshape(YS * rows, cols)
    h_t = h.T
    h_own = lax.dynamic_slice(h_t, (x * share, 0), (share, YS * rows))
    h_others = lax.dynamic_update_slice(h_t, jnp.zeros_like(h_own), (x * share, 0))
    others, own = down_parts(every, h_others, h_own, w_cols, width)
    others = lax.psum_scatter(others, "x", scatter_dimension=0, tiled=True)
    d_down = own + others.astype(F32)

    back = hidden_parts(every, w_cols, h, width, wide)
    back = lax.all_to_all(
        back.reshape(YS, rows, wide), "y", split_axis=0, concat_axis=0, tiled=True
    )
    d_hidden = back[:, :, :cols].transpose(1, 0, 2).reshape(hidden.shape)
    d_slot = jnp.sum(back[:, :, cols : cols + 2].astype(F32), axis=(0, 2))
    returned = lax.all_to_all(
        d_slot.reshape(nexp, cap), "expert", split_axis=0, concat_axis=0, tiled=True
    )

    flat = routes.reshape(-1)
    onehot = (flat[:, None] == jnp.arange(nexp, dtype=jnp.int32)[None, :]).astype(jnp.int32)
    before = jnp.cumsum(onehot, axis=0) - onehot
    slot = jnp.sum(before * onehot, axis=1)
    select = (flat * cap + slot)[:, None] == jnp.arange(rows, dtype=jnp.int32)[None, :]
    d_probs = jnp.sum(jnp.where(select, returned.reshape(-1)[None, :], 0.0), axis=1)
    return d_probs.reshape(tok, topk), d_hidden, d_down.reshape(w_down.shape)


def solution(mesh):
    grid = Mesh(mesh.devices.reshape(YS, XS, -1), ("y", "x", "expert"))
    tokens = P(("y", "x", "expert"), None)
    saved = P(("y", "x"), "expert", None, None, None)
    weight = P("expert", ("y", "x"), None)
    return jax.shard_map(
        body,
        mesh=grid,
        in_specs=(tokens, tokens, tokens, saved, weight),
        out_specs=(tokens, saved, weight),
        check_vma=False,
    )
```

time: 185 us -> 161 us (0.87); the launches traced: 183 us -> 161 us
  matrix products: 14.5 us -> 0 us
  Pallas kernels: 0 us -> 14.2 us
  waiting for transfers between devices: 40.2 us -> 53.4 us
  starting transfers between devices: 42.4 us -> 29.6 us
  local copies, waits for them, and re-layouts: 31.6 us -> 19.8 us
  other arithmetic: 15.5 us -> 4.17 us
    all_gather x0 -> x1, blocking collectives: none -> 25.4 us  [body(): lax.all_gather(pack(grad_out, routes, probs, me.reshape(1)), 'expert', ax...]
    all_to_all x1 -> x0, blocking collectives: 24.2 us -> none  [body(): lax.all_to_all(send, 'expert', split_axis=0, concat_axis=0, tiled=True)]
    dot_general x6 -> x0, matrix products: 14.5 us -> none  [the longest x4 8.82 us: part(): return jnp.dot(block, g, preferred_element_type=F32)]
    pallas_call x0 -> x4, Pallas kernels: none -> 14.2 us  [the longest x1 6.67 us: hidden_parts(): pl.pallas_call(kernel, grid=(steps,), out_shape=jax.ShapeDtypeStruct((row...]
    ppermute x8 -> x4, waiting for transfers between devices: 13.9 us -> 26.8 us  [shift(): return lax.ppermute(a, 'x', [(i, (i + step) % XS) for i in range(XS)])]
    ppermute x8 -> x4, starting transfers between devices: 23.3 us -> 11.7 us  [shift(): return lax.ppermute(a, 'x', [(i, (i + step) % XS) for i in range(XS)])]
    all_gather x1, waiting for transfers between devices: 9.54 us -> 0.01 us  [body(): every = lax.all_gather(mine, 'y', axis=0, tiled=True)]
    all_to_all x2, waiting for transfers between devices: 12.7 us -> 21.3 us  [the longest x1 21.2 us: body(): lax.all_to_all(back.reshape(YS, rows, wide), 'y', split_axis=0, concat_ax...]
  transfers between devices with their start and end apart: 12 -> 9, of which waited for: 6 -> 5; matrix products, arithmetic and copies ran while one was open for 21% -> 10% of each run, Pallas kernels for 0% -> 4%
where the time goes in v2:
time: 161 us
  waiting for transfers between devices  53.4 us (33%)
  starting transfers between devices  29.6 us (18%)
  blocking collectives  25.4 us (16%)
  local copies, waits for them, and re-layouts  19.8 us (12%)
  between operations  14.3 us (9%)
  Pallas kernels  14.2 us (9%)
  other arithmetic  4.17 us (3%)
    ppermute x4, waiting for transfers between devices, shift(): return lax.ppermute(a, 'x', [(i, (i + step) % XS) for i in range(XS)])  26.8 us
    all_gather x1, blocking collectives, body(): lax.all_gather(pack(grad_out, routes, probs, me.reshape(1)), 'expert', ax...  25.4 us
    all_to_all x1, waiting for transfers between devices, body(): lax.all_to_all(back.reshape(YS, rows, wide), 'y', split_axis=0, concat_ax...  21.2 us
    ppermute x4, starting transfers between devices, shift(): return lax.ppermute(a, 'x', [(i, (i + step) % XS) for i in range(XS)])  11.7 us
    all_to_all x1, starting transfers between devices, body(): lax.all_to_all(back.reshape(YS, rows, wide), 'y', split_axis=0, concat_ax...  7.29 us
    all_to_all x1, starting transfers between devices, body(): h = lax.all_to_all(h, 'y', split_axis=0, concat_axis=0, tiled=True)  7.1 us
    dynamic_update_slice x5, local copies, waits for them, and re-layouts, gather_w(): lax.dynamic_update_slice(o, v, ((x + step) % XS * n + low, 0))  6.88 us
    pallas_call x1, Pallas kernels, hidden_parts(): pl.pallas_call(kernel, grid=(steps,), out_shape=jax.ShapeDtypeStruct((row...  6.67 us
  transfers between devices with their start and end apart: 9, of which 5 were waited for; matrix products, arithmetic and copies ran while one was open for 10% of the time, Pallas kernels for 4%

profile of v2, /device:TPU:6, one launch (start us, length us, event | category | flops | bytes accessed | tf_op | source)
XLA Modules:
  0.0 160.9 jit_solution(14411919844373492119)
XLA Ops:
  7.2 2.5 %reshape.58 = bf16[16,4,8,672]{3,2,1,0:T(8,128)(2,1)S(1)} reshape(bf16[1,1,16,4,5376]{4,3,2,1,0:T(4,128)(2,1)} %param.8) | data formatting | bytes 1376256 | tf_op jit(solution)/shard_map/reshape | solution.py:199
  9.7 1.2 copy.39
  10.8 7.1 %all-to-all-start = ((bf16[8,16,4,672]{3,2,1,0:T(4,128)(2,1)}), bf16[8,16,4,672]{3,2,1,0:T(4,128)(2,1)S(1)}, u32[]{:S(2)}, u32[]{:S(2)}) async-start(bf16[8,16,4,672]{3,2,1,0:T(4,128)(2,1)} %bitcast.16), calls=%async_computation | async-start | bytes 1572864 | tf_op jit(solution)/shard_map/all_to_all | solution.py:200
  17.9 0.0 all-gather.2.cloned.1.call-start
  18.0 0.1 pack_tokens.1
  18.1 25.4 %all_gather.6.refs_1_ = bf16[128,3200]{1,0:T(8,128)(2,1)S(1)} all-gather(bf16[8,3200]{1,0:T(8,128)(2,1)S(1)} %pack_tokens.1), channel_id=1, replica_groups=mesh['y'=8,'x'=4,'expert'=16] {'expert'}, dimensions={0}, use_global_device_ids=true | all-gather | bytes 870400 | tf_op jit(solution)/shard_map/all_gather | solution.py:202
  43.5 1.2 pick_slots.1
  44.7 0.0 reduce-scatter.2.cloned.1.call-start
  44.8 2.4 %collective-permute-start = (bf16[168,3072]{1,0:T(8,128)(2,1)}, bf16[168,3072]{1,0:T(8,128)(2,1)S(1)}, u32[]{:S(2)}, u32[]{:S(2)}) collective-permute-start(bf16[168,3072]{1,0:T(8,128)(2,1)} %bitcast.21), channel_id=1, source_target_pairs={{0,16},{16,32},{32,48},{48,0},{1,17},{17,33},{33,49},{49,1},{2,18}... | collective-permute-start | bytes 3096584 | tf_op jit(solution)/shard_map/ppermute | solution.py:19
  47.2 3.5 %collective-permute-start.1 = (bf16[168,3072]{1,0:T(8,128)(2,1)}, bf16[168,3072]{1,0:T(8,128)(2,1)S(1)}, u32[]{:S(2)}, u32[]{:S(2)}) collective-permute-start(bf16[168,3072]{1,0:T(8,128)(2,1)} %bitcast.22), channel_id=1, source_target_pairs={{0,48},{16,0},{32,16},{48,32},{1,49},{17,1},{33,17},{49,33},{2,50}... | collective-permute-start | bytes 3096584 | tf_op jit(solution)/shard_map/ppermute | solution.py:19
  50.7 2.5 %broadcast_in_dim.23 = bf16[672,3072]{1,0:T(8,128)(2,1)} broadcast(bf16[]{:T(256)} %constant.49.clone.1), dimensions={} | broadcast | bytes 4128770 | tf_op jit(solution)/shard_map/broadcast_in_dim | solution.py:27
  53.2 1.0 constant_dynamic-update-slice_fusion.4
  54.2 17.7 %collective-permute-done = bf16[168,3072]{1,0:T(8,128)(2,1)S(1)} collective-permute-done((bf16[168,3072]{1,0:T(8,128)(2,1)}, bf16[168,3072]{1,0:T(8,128)(2,1)S(1)}, u32[]{:S(2)}, u32[]{:S(2)}) %collective-permute-start) | collective-permute-done | bytes 1032224 | tf_op jit(solution)/shard_map/ppermute | solution.py:19
  71.9 0.8 slice.16
  72.7 3.6 %collective-permute-start.2 = (bf16[80,3072]{1,0:T(8,128)(2,1)}, bf16[80,3072]{1,0:T(8,128)(2,1)}, u32[]{:S(2)}, u32[]{:S(2)}) collective-permute-start(bf16[80,3072]{1,0:T(8,128)(2,1)} %slice.16), channel_id=1, source_target_pairs={{0,16},{16,32},{32,48},{48,0},{1,17},{17,33},{33,49},{49,1},{2,18}... | collective-permute-start | bytes 1474568 | tf_op jit(solution)/shard_map/ppermute | solution.py:19
  76.4 2.2 %collective-permute-start.3 = (bf16[88,3072]{1,0:T(8,128)(2,1)S(1)}, bf16[88,3072]{1,0:T(8,128)(2,1)}, u32[]{:S(2)}, u32[]{:S(2)}) collective-permute-start(bf16[88,3072]{1,0:T(8,128)(2,1)S(1)} %slice.17), channel_id=1, source_target_pairs={{0,48},{16,0},{32,16},{48,32},{1,49},{17,1},{33,17},{49,33},{2,50}... | collective-permute-start | bytes 1622024 | tf_op jit(solution)/shard_map/ppermute | solution.py:19
  78.6 1.1 constant_dynamic-update-slice_fusion.3
  79.7 1.0 constant_dynamic-update-slice_fusion.2
  80.7 0.4 reshape.53.h_ref
  81.1 0.3 copy.33
  81.4 0.7 dynamic-slice_bitcast_fusion.mine_ref
  82.2 5.5 %collective-permute-done.2 = bf16[80,3072]{1,0:T(8,128)(2,1)} collective-permute-done((bf16[80,3072]{1,0:T(8,128)(2,1)}, bf16[80,3072]{1,0:T(8,128)(2,1)}, u32[]{:S(2)}, u32[]{:S(2)}) %collective-permute-start.2) | collective-permute-done | bytes 491552 | tf_op jit(solution)/shard_map/ppermute | solution.py:19
  87.7 1.9 %constant_dynamic-update-slice_fusion.1 = bf16[672,3072]{1,0:T(8,128)(2,1)} fusion(bf16[672,3072]{1,0:T(8,128)(2,1)} %constant_dynamic-update-slice_fusion.2, bf16[80,3072]{1,0:T(8,128)(2,1)} %collective-permute-done.2, s32[]{:T(128)S(6)} %select_n.51), kind=kLoop, calls=%fused_computation.12 | loop fusion | bytes 983044 | tf_op jit(solution)/shard_map/dynamic_update_slice | solution.py:28
  89.6 3.6 %collective-permute-done.3 = bf16[88,3072]{1,0:T(8,128)(2,1)} collective-permute-done((bf16[88,3072]{1,0:T(8,128)(2,1)S(1)}, bf16[88,3072]{1,0:T(8,128)(2,1)}, u32[]{:S(2)}, u32[]{:S(2)}) %collective-permute-start.3) | collective-permute-done | bytes 540704 | tf_op jit(solution)/shard_map/ppermute | solution.py:19
  93.2 1.9 %constant_dynamic-update-slice_fusion.w_ref._ = bf16[672,3072]{1,0:T(8,128)(2,1)} fusion(bf16[672,3072]{1,0:T(8,128)(2,1)} %constant_dynamic-update-slice_fusion.1, bf16[88,3072]{1,0:T(8,128)(2,1)} %collective-permute-done.3, s32[]{:T(128)S(6)} %select_n.52), kind=kLoop, calls=%fused_computation.11 | loop fusion | bytes 1081348 | tf_op jit(solution)/shard_map/dynamic_update_slice | solution.py:28
  95.1 6.3 %down_parts.1 = (bf16[672,3072]{1,0:T(8,128)(2,1)}, f32[168,3072]{1,0:T(8,128)}) custom-call(bf16[512,3200]{1,0:T(8,128)(2,1)} %all-gather.2.cloned.1.call-done.dy_ref.p_ref, bf16[512,3200]{1,0:T(8,128)(2,1)} %all-gather.2.cloned.1.call-done.dy_ref.p_ref, bf16[672,512]{1,0:T(8,128)(2,1)} %copy-done.4, bf16[168,512]{1,0:T(8,128)(2,1)} %dynamic-slice_bitcast_fusion.mine_ref, ...), custom_call_target="tpu_custom_call" | custom-call | flops 2113929216 | bytes 12000000 | tf_op jit(solution)/shard_map/down_parts/pallas_call | solution.py:113
  101.4 6.7 %hidden_parts.1 = bf16[512,768]{1,0:T(8,128)(2,1)} custom-call(bf16[512,3200]{1,0:T(8,128)(2,1)} %all-gather.2.cloned.1.call-done.dy_ref.p_ref, bf16[512,3200]{1,0:T(8,128)(2,1)} %all-gather.2.cloned.1.call-done.dy_ref.p_ref, bf16[672,3072]{1,0:T(8,128)(2,1)} %constant_dynamic-update-slice_fusion.w_ref._, bf16[512,672]{1,0:T(8,128)(2,1)} %copy-done.3), custom_call_target="tpu_custom_call" | custom-call | flops 2113929216 | bytes 9000000 | tf_op jit(solution)/shard_map/hidden_parts/pallas_call | solution.py:167
  108.0 7.3 %all-to-all-start.1 = ((bf16[8,64,768]{2,1,0:T(8,128)(2,1)}), bf16[8,64,768]{2,1,0:T(8,128)(2,1)S(1)}, u32[]{:S(2)}, u32[]{:S(2)}) async-start(bf16[8,64,768]{2,1,0:T(8,128)(2,1)} %bitcast.20), calls=%async_computation.1 | async-start | bytes 1572864 | tf_op jit(solution)/shard_map/all_to_all | solution.py:216
  115.3 0.1 copy.28
  115.4 0.1 reshape.49
  115.5 0.1 fusion
  115.6 0.1 reduce_window_sum.11
  115.6 0.2 select_reduce_fusion.1
  115.8 21.2 %all-to-all-done.1 = bf16[8,64,768]{2,1,0:T(8,128)(2,1)S(1)} async-done(((bf16[8,64,768]{2,1,0:T(8,128)(2,1)}), bf16[8,64,768]{2,1,0:T(8,128)(2,1)S(1)}, u32[]{:S(2)}, u32[]{:S(2)}) %all-to-all-start.1) | async-done | bytes 786464 | tf_op jit(solution)/shard_map/all_to_all | solution.py:216
  137.1 0.2 convert_reduce_fusion
  137.3 0.7 all_to_all.14
  138.0 3.5 %all-to-all-start.2 = ((f32[16,1,4]{2,1,0:T(1,128)}), f32[16,1,4]{2,1,0:T(1,128)S(1)}, u32[]{:S(2)}, u32[]{:S(2)}) async-start(f32[16,1,4]{2,1,0:T(1,128)} %bitcast.6), calls=%async_computation.2 | async-start | bytes 16384 | tf_op jit(solution)/shard_map/all_to_all | solution.py:221
  141.4 0.1 slice_bitcast_fusion
  141.5 0.4 copy.32
  142.0 1.8 %reshape.56 = bf16[1,1,16,4,5376]{4,3,2,1,0:T(4,128)(2,1)} reshape(bf16[64,8,672]{2,1,0:T(8,128)(2,1)S(1)} %copy.32) | data formatting | bytes 1376256 | tf_op jit(solution)/shard_map/reshape | solution.py:219
  143.8 5.2 %all-to-all-done.2 = f32[16,1,4]{2,1,0:T(1,128)S(1)} async-done(((f32[16,1,4]{2,1,0:T(1,128)}), f32[16,1,4]{2,1,0:T(1,128)S(1)}, u32[]{:S(2)}, u32[]{:S(2)}) %all-to-all-start.2) | async-done | bytes 288 | tf_op jit(solution)/shard_map/all_to_all | solution.py:221
  149.0 0.5 broadcast.16
  149.5 0.7 reduce.3
  150.2 0.1 broadcast_in_dim.24
  150.3 0.2 select_reduce_fusion
  150.5 0.1 reshape.55
  150.6 0.7 copy.35
  151.2 2.8 %add_bitcast_fusion = f32[1,168,3072]{2,1,0:T(8,128)} fusion(f32[168,3072]{1,0:T(8,128)S(1)} %copy-done.5, bf16[168,3072]{1,0:T(8,128)(2,1)} %reduce-scatter.2.cloned.1.call-done), kind=kLoop, calls=%fused_computation | loop fusion | flops 1032192 | bytes 5160960 | tf_op jit(solution)/shard_map/reshape | solution.py:231
  (23 shorter events, 0.1 us)
Async XLA Ops:
  7.2 10.8 %copy-start = (bf16[8,3072]{1,0:T(8,128)(2,1)S(1)}, bf16[8,3072]{1,0:T(8,128)(2,1)}, u32[]{:S(2)}) copy-start(bf16[8,3072]{1,0:T(8,128)(2,1)} %dy_ref.1) | copy-start | bytes 147460
  7.2 10.8 %copy-start.1 = (s32[8,4]{0,1:T(4,128)S(1)}, s32[8,4]{0,1:T(4,128)}, u32[]{:S(2)}) copy-start(s32[8,4]{0,1:T(4,128)} %param.6) | copy-start | bytes 388
  7.2 10.8 %copy-start.2 = (bf16[8,4]{0,1:T(4,128)(2,1)S(1)}, bf16[8,4]{0,1:T(4,128)(2,1)}, u32[]{:S(2)}) copy-start(bf16[8,4]{0,1:T(4,128)(2,1)} %param.7) | copy-start | bytes 196
  10.8 32.7 %all-to-all-start = ((bf16[8,16,4,672]{3,2,1,0:T(4,128)(2,1)}), bf16[8,16,4,672]{3,2,1,0:T(4,128)(2,1)S(1)}, u32[]{:S(2)}, u32[]{:S(2)}) async-start(bf16[8,16,4,672]{3,2,1,0:T(4,128)(2,1)} %bitcast.16), calls=%async_computation | async-start | bytes 1572864 | tf_op jit(solution)/shard_map/all_to_all | solution.py:200
  17.9 77.1 %all-gather.2.cloned.1.call-start = ((), (), s32[]{:S(2)}) async-start(), calls=%async_computation.4 | async-start | bytes 3686400 | tf_op jit(solution)/shard_map/all_gather | solution.py:204
  44.7 106.5 %reduce-scatter.2.cloned.1.call-start = ((), (), s32[]{:S(2)}) async-start(), calls=%async_computation.5 | async-start | bytes 5160960 | tf_op jit(solution)/shard_map/reduce_scatter | solution.py:212
  44.8 27.2 %collective-permute-start = (bf16[168,3072]{1,0:T(8,128)(2,1)}, bf16[168,3072]{1,0:T(8,128)(2,1)S(1)}, u32[]{:S(2)}, u32[]{:S(2)}) collective-permute-start(bf16[168,3072]{1,0:T(8,128)(2,1)} %bitcast.21), channel_id=1, source_target_pairs={{0,16},{16,32},{32,48},{48,0},{1,17},{17,33},{33,49},{49,1},{2,18}... | collective-permute-start | bytes 3096584 | tf_op jit(solution)/shard_map/ppermute | solution.py:19
  47.2 29.2 %collective-permute-start.1 = (bf16[168,3072]{1,0:T(8,128)(2,1)}, bf16[168,3072]{1,0:T(8,128)(2,1)S(1)}, u32[]{:S(2)}, u32[]{:S(2)}) collective-permute-start(bf16[168,3072]{1,0:T(8,128)(2,1)} %bitcast.22), channel_id=1, source_target_pairs={{0,48},{16,0},{32,16},{48,32},{1,49},{17,1},{33,17},{49,33},{2,50}... | collective-permute-start | bytes 3096584 | tf_op jit(solution)/shard_map/ppermute | solution.py:19
  50.7 2.5 %copy-start.6 = (bf16[1,168,3072]{2,1,0:T(8,128)(2,1)S(1)}, bf16[1,168,3072]{2,1,0:T(8,128)(2,1)}, u32[]{:S(2)}) copy-start(bf16[1,168,3072]{2,1,0:T(8,128)(2,1)} %param.9) | copy-start | bytes 3096580
  72.7 15.0 %collective-permute-start.2 = (bf16[80,3072]{1,0:T(8,128)(2,1)}, bf16[80,3072]{1,0:T(8,128)(2,1)}, u32[]{:S(2)}, u32[]{:S(2)}) collective-permute-start(bf16[80,3072]{1,0:T(8,128)(2,1)} %slice.16), channel_id=1, source_target_pairs={{0,16},{16,32},{32,48},{48,0},{1,17},{17,33},{33,49},{49,1},{2,18}... | collective-permute-start | bytes 1474568 | tf_op jit(solution)/shard_map/ppermute | solution.py:19
  76.4 16.8 %collective-permute-start.3 = (bf16[88,3072]{1,0:T(8,128)(2,1)S(1)}, bf16[88,3072]{1,0:T(8,128)(2,1)}, u32[]{:S(2)}, u32[]{:S(2)}) collective-permute-start(bf16[88,3072]{1,0:T(8,128)(2,1)S(1)} %slice.17), channel_id=1, source_target_pairs={{0,48},{16,0},{32,16},{48,32},{1,49},{17,1},{33,17},{49,33},{2,50}... | collective-permute-start | bytes 1622024 | tf_op jit(solution)/shard_map/ppermute | solution.py:19
  81.1 20.2 %copy-start.3 = (bf16[512,672]{1,0:T(8,128)(2,1)}, bf16[512,672]{1,0:T(8,128)(2,1)S(1)}, u32[]{:S(2)}) copy-start(bf16[512,672]{1,0:T(8,128)(2,1)S(1)} %reshape.53.h_ref) | copy-start | bytes 2064388
  82.2 12.9 %copy-start.4 = (bf16[672,512]{1,0:T(8,128)(2,1)}, bf16[672,512]{1,0:T(8,128)(2,1)S(1)}, u32[]{:S(2)}) copy-start(bf16[672,512]{1,0:T(8,128)(2,1)S(1)} %broadcast_dynamic-update-slice_fusion.others_ref) | copy-start | bytes 2064388
  108.0 43.2 %copy-start.5 = (f32[168,3072]{1,0:T(8,128)S(1)}, f32[168,3072]{1,0:T(8,128)}, u32[]{:S(2)}) copy-start(f32[168,3072]{1,0:T(8,128)} %get-tuple-element.5) | copy-start | bytes 6193156
  108.0 29.0 %all-to-all-start.1 = ((bf16[8,64,768]{2,1,0:T(8,128)(2,1)}), bf16[8,64,768]{2,1,0:T(8,128)(2,1)S(1)}, u32[]{:S(2)}, u32[]{:S(2)}) async-start(bf16[8,64,768]{2,1,0:T(8,128)(2,1)} %bitcast.20), calls=%async_computation.1 | async-start | bytes 1572864 | tf_op jit(solution)/shard_map/all_to_all | solution.py:216
  138.0 11.1 %all-to-all-start.2 = ((f32[16,1,4]{2,1,0:T(1,128)}), f32[16,1,4]{2,1,0:T(1,128)S(1)}, u32[]{:S(2)}, u32[]{:S(2)}) async-start(f32[16,1,4]{2,1,0:T(1,128)} %bitcast.6), calls=%async_computation.2 | async-start | bytes 16384 | tf_op jit(solution)/shard_map/all_to_all | solution.py:221
Sparse Core Ops, SparseCore 0:
  44.8 45.5 all-gather.1
  101.5 46.5 reduce-scatter.1

commit v3 on v2

--- a/solution.py
+++ b/solution.py
@@ -11,7 +11,7 @@
 TILE = 1536
 
 
-def params(mib=60):
+def params(mib=52):
     return pltpu.CompilerParams(vmem_limit_bytes=mib * 1024 * 1024)
 
 
@@ -184,6 +184,39 @@
     )(every, every, w_cols, h)
 
 
+def pick_probs(routes, values):
+    tok, topk = routes.shape
+    nexp, cap = values.shape
+
+    def kernel(r_ref, v_ref, out_ref):
+        fill = jnp.full((topk, LANES - tok), -1, jnp.int32)
+        route = jnp.concatenate([r_ref[...], fill], axis=1)
+        expert = lax.broadcasted_iota(jnp.int32, (nexp, LANES), 0)
+        hits = [route[k : k + 1] == expert for k in range(topk)]
+        chosen = sum(hit.astype(F32) for hit in hits)
+        older = lax.broadcasted_iota(jnp.int32, (LANES, LANES), 0)
+        newer = lax.broadcasted_iota(jnp.int32, (LANES, LANES), 1)
+        slot = jnp.dot(
+            chosen.astype(BF16), (older < newer).astype(BF16), preferred_element_type=F32
+        )
+        value = jnp.zeros((nexp, LANES), F32)
+        for c in range(cap):
+            value = jnp.where(slot == c, v_ref[:, c : c + 1], value)
+        found = [jnp.sum(jnp.where(hit, value, 0.0), axis=0, keepdims=True) for hit in hits]
+        out_ref[...] = jnp.concatenate(found, axis=0)[:, :tok]
+
+    vmem = pl.BlockSpec(memory_space=pltpu.VMEM)
+    return pl.pallas_call(
+        kernel,
+        out_shape=jax.ShapeDtypeStruct((topk, tok), F32),
+        in_specs=[vmem, vmem],
+        out_specs=vmem,
+        compiler_params=params(16),
+        cost_estimate=pl.CostEstimate(flops=0, bytes_accessed=20000, transcendentals=0),
+        name="pick_probs",
+    )(routes.T, values)
+
+
 def body(grad_out, routes, probs, hidden, w_down):
     tok, width = grad_out.shape
     topk = routes.shape[1]
@@ -222,13 +255,8 @@
         d_slot.reshape(nexp, cap), "expert", split_axis=0, concat_axis=0, tiled=True
     )
 
-    flat = routes.reshape(-1)
-    onehot = (flat[:, None] == jnp.arange(nexp, dtype=jnp.int32)[None, :]).astype(jnp.int32)
-    before = jnp.cumsum(onehot, axis=0) - onehot
-    slot = jnp.sum(before * onehot, axis=1)
-    select = (flat * cap + slot)[:, None] == jnp.arange(rows, dtype=jnp.int32)[None, :]
-    d_probs = jnp.sum(jnp.where(select, returned.reshape(-1)[None, :], 0.0), axis=1)
-    return d_probs.reshape(tok, topk), d_hidden, d_down.reshape(w_down.shape)
+    d_probs = pick_probs(routes, returned.reshape(nexp, cap)).T
+    return d_probs, d_hidden, d_down.reshape(w_down.shape)
 
 
 def solution(mesh):

time: 161 us -> 161 us (level); the launches traced: 161 us -> 157 us
  blocking collectives: 25.4 us -> 54.1 us
  waiting for transfers between devices: 53.4 us -> 32.2 us
  starting transfers between devices: 29.6 us -> 22.3 us
  local copies, waits for them, and re-layouts: 19.8 us -> 17.9 us
    all_to_all x0 -> x1, blocking collectives: none -> 28.7 us  [body(): lax.all_to_all(back.reshape(YS, rows, wide), 'y', split_axis=0, concat_ax...]
    all_to_all x1 -> x0, waiting for transfers between devices: 21.2 us -> none  [body(): lax.all_to_all(back.reshape(YS, rows, wide), 'y', split_axis=0, concat_ax...]
    all_to_all x1 -> x0, starting transfers between devices: 7.29 us -> none  [body(): lax.all_to_all(back.reshape(YS, rows, wide), 'y', split_axis=0, concat_ax...]
  transfers between devices with their start and end apart: 9 -> 8, of which waited for: 5 -> 4; matrix products, arithmetic and copies ran while one was open for 10% -> 9% of each run, Pallas kernels for 4% -> 4%
where the time goes in v3:
time: 161 us; the launch traced here: 157 us
  blocking collectives  54.1 us (34%)
  waiting for transfers between devices  32.2 us (20%)
  starting transfers between devices  22.3 us (14%)
  local copies, waits for them, and re-layouts  17.9 us (11%)
  between operations  14.3 us (9%)
  Pallas kernels  13.6 us (8%)
  other arithmetic  3 us (2%)
    all_to_all x1, blocking collectives, body(): lax.all_to_all(back.reshape(YS, rows, wide), 'y', split_axis=0, concat_ax...  28.7 us
    ppermute x4, waiting for transfers between devices, shift(): return lax.ppermute(a, 'x', [(i, (i + step) % XS) for i in range(XS)])  27 us
    all_gather x1, blocking collectives, body(): lax.all_gather(pack(grad_out, routes, probs, me.reshape(1)), 'expert', ax...  25.4 us
    ppermute x4, starting transfers between devices, shift(): return lax.ppermute(a, 'x', [(i, (i + step) % XS) for i in range(XS)])  11.7 us
    all_to_all x1, starting transfers between devices, body(): h = lax.all_to_all(h, 'y', split_axis=0, concat_axis=0, tiled=True)  7.1 us
    pallas_call x1, Pallas kernels, down_parts(): pl.pallas_call(kernel, grid=(width // TILE,), out_shape=(jax.ShapeDtypeSt...  6.08 us
    dynamic_update_slice x5, local copies, waits for them, and re-layouts, gather_w(): lax.dynamic_update_slice(o, v, ((x + step) % XS * n + low, 0))  6.05 us
    pallas_call x1, Pallas kernels, hidden_parts(): pl.pallas_call(kernel, grid=(steps,), out_shape=jax.ShapeDtypeStruct((row...  5.59 us
  transfers between devices with their start and end apart: 8, of which 4 were waited for; matrix products, arithmetic and copies ran while one was open for 9% of the time, Pallas kernels for 4%

profile of v3, /device:TPU:6, one launch (start us, length us, event | category | flops | bytes accessed | tf_op | source)
XLA Modules:
  0.0 157.5 jit_solution(2280339322899244187)
XLA Ops:
  7.2 0.0 copy-start.1
  7.2 0.0 copy-start
  7.2 0.0 copy-start.2
  7.2 0.0 copy-start.4
  7.2 2.5 %reshape.39 = bf16[16,4,8,672]{3,2,1,0:T(8,128)(2,1)S(1)} reshape(bf16[1,1,16,4,5376]{4,3,2,1,0:T(4,128)(2,1)} %param.8) | data formatting | bytes 1376256 | tf_op jit(solution)/shard_map/reshape | solution.py:232
  9.7 1.2 copy.32
  10.9 7.1 %all-to-all-start = ((bf16[8,16,4,672]{3,2,1,0:T(4,128)(2,1)}), bf16[8,16,4,672]{3,2,1,0:T(4,128)(2,1)S(1)}, u32[]{:S(2)}, u32[]{:S(2)}) async-start(bf16[8,16,4,672]{3,2,1,0:T(4,128)(2,1)} %bitcast.18), calls=%async_computation | async-start | bytes 1572864 | tf_op jit(solution)/shard_map/all_to_all | solution.py:233
  18.0 0.0 all-gather.2.cloned.1.call-start
  18.1 0.0 copy-done.1
  18.1 0.0 copy-done
  18.1 0.0 copy-done.2
  18.1 0.1 pack_tokens.1
  18.2 25.4 %all_gather.6.refs_1_ = bf16[128,3200]{1,0:T(8,128)(2,1)S(1)} all-gather(bf16[8,3200]{1,0:T(8,128)(2,1)S(1)} %pack_tokens.1), channel_id=1, replica_groups=mesh['y'=8,'x'=4,'expert'=16] {'expert'}, dimensions={0}, use_global_device_ids=true | all-gather | bytes 870400 | tf_op jit(solution)/shard_map/all_gather | solution.py:235
  43.6 0.0 all-to-all-done.refs_2_
  43.6 1.2 pick_slots.1
  44.8 0.0 all-gather.2.cloned.1.call-update
  44.8 0.0 reduce-scatter.2.cloned.1.call-start
  44.8 2.4 %collective-permute-start = (bf16[168,3072]{1,0:T(8,128)(2,1)S(1)}, bf16[168,3072]{1,0:T(8,128)(2,1)}, u32[]{:S(2)}, u32[]{:S(2)}) collective-permute-start(bf16[168,3072]{1,0:T(8,128)(2,1)S(1)} %bitcast.25), channel_id=1, source_target_pairs={{0,16},{16,32},{32,48},{48,0},{1,17},{17,33},{33,49},{49,1},{2,18}... | collective-permute-start | bytes 3096584 | tf_op jit(solution)/shard_map/ppermute | solution.py:19
  47.2 3.5 %collective-permute-start.1 = (bf16[168,3072]{1,0:T(8,128)(2,1)S(1)}, bf16[168,3072]{1,0:T(8,128)(2,1)S(1)}, u32[]{:S(2)}, u32[]{:S(2)}) collective-permute-start(bf16[168,3072]{1,0:T(8,128)(2,1)S(1)} %bitcast.26), channel_id=1, source_target_pairs={{0,48},{16,0},{32,16},{48,32},{1,49},{17,1},{33,17},{49,33},{2,50}... | collective-permute-start | bytes 3096584 | tf_op jit(solution)/shard_map/ppermute | solution.py:19
  50.8 2.5 %broadcast_in_dim.6 = bf16[672,3072]{1,0:T(8,128)(2,1)} broadcast(bf16[]{:T(256)} %constant.42.clone.1), dimensions={} | broadcast | bytes 4128770 | tf_op jit(solution)/shard_map/broadcast_in_dim | solution.py:27
  53.2 1.1 constant_dynamic-update-slice_fusion.4
  54.3 17.6 %collective-permute-done = bf16[168,3072]{1,0:T(8,128)(2,1)} collective-permute-done((bf16[168,3072]{1,0:T(8,128)(2,1)S(1)}, bf16[168,3072]{1,0:T(8,128)(2,1)}, u32[]{:S(2)}, u32[]{:S(2)}) %collective-permute-start) | collective-permute-done | bytes 1032224 | tf_op jit(solution)/shard_map/ppermute | solution.py:19
  71.9 1.8 %slice.16 = bf16[80,3072]{1,0:T(8,128)(2,1)} slice(bf16[168,3072]{1,0:T(8,128)(2,1)} %collective-permute-done), slice={[0:80], [0:3072]} | slice | bytes 983040 | tf_op jit(solution)/shard_map/slice | solution.py:26
  73.8 3.6 %collective-permute-start.2 = (bf16[80,3072]{1,0:T(8,128)(2,1)}, bf16[80,3072]{1,0:T(8,128)(2,1)S(1)}, u32[]{:S(2)}, u32[]{:S(2)}) collective-permute-start(bf16[80,3072]{1,0:T(8,128)(2,1)} %slice.16), channel_id=1, source_target_pairs={{0,16},{16,32},{32,48},{48,0},{1,17},{17,33},{33,49},{49,1},{2,18}... | collective-permute-start | bytes 1474568 | tf_op jit(solution)/shard_map/ppermute | solution.py:19
  77.3 0.0 collective-permute-done.1
  77.4 2.2 %collective-permute-start.3 = (bf16[88,3072]{1,0:T(8,128)(2,1)S(1)}, bf16[88,3072]{1,0:T(8,128)(2,1)S(1)}, u32[]{:S(2)}, u32[]{:S(2)}) collective-permute-start(bf16[88,3072]{1,0:T(8,128)(2,1)S(1)} %slice.17), channel_id=1, source_target_pairs={{0,48},{16,0},{32,16},{48,32},{1,49},{17,1},{33,17},{49,33},{2,50}... | collective-permute-start | bytes 1622024 | tf_op jit(solution)/shard_map/ppermute | solution.py:19
  79.7 2.3 %constant_dynamic-update-slice_fusion.3 = bf16[672,3072]{1,0:T(8,128)(2,1)} fusion(bf16[672,3072]{1,0:T(8,128)(2,1)} %constant_dynamic-update-slice_fusion.4, bf16[168,3072]{1,0:T(8,128)(2,1)} %collective-permute-done, s32[]{:T(128)S(6)} %select_n.43), kind=kLoop, calls=%fused_computation.9 | loop fusion | bytes 2064388 | tf_op jit(solution)/shard_map/dynamic_update_slice | solution.py:28
  82.0 1.0 constant_dynamic-update-slice_fusion.2
  83.0 0.4 reshape.35.h_ref
  83.4 0.3 copy.26
  83.7 4.8 %collective-permute-done.2 = bf16[80,3072]{1,0:T(8,128)(2,1)S(1)} collective-permute-done((bf16[80,3072]{1,0:T(8,128)(2,1)}, bf16[80,3072]{1,0:T(8,128)(2,1)S(1)}, u32[]{:S(2)}, u32[]{:S(2)}) %collective-permute-start.2) | collective-permute-done | bytes 491552 | tf_op jit(solution)/shard_map/ppermute | solution.py:19
  88.5 0.8 constant_dynamic-update-slice_fusion.1
  89.4 4.6 %collective-permute-done.3 = bf16[88,3072]{1,0:T(8,128)(2,1)S(1)} collective-permute-done((bf16[88,3072]{1,0:T(8,128)(2,1)S(1)}, bf16[88,3072]{1,0:T(8,128)(2,1)S(1)}, u32[]{:S(2)}, u32[]{:S(2)}) %collective-permute-start.3) | collective-permute-done | bytes 540704 | tf_op jit(solution)/shard_map/ppermute | solution.py:19
  94.0 0.8 constant_dynamic-update-slice_fusion.w_ref._
  94.8 6.1 %down_parts.1 = (bf16[672,3072]{1,0:T(8,128)(2,1)}, f32[168,3072]{1,0:T(8,128)}) custom-call(bf16[512,3200]{1,0:T(8,128)(2,1)} %all-gather.2.cloned.1.call-done.dy_ref.p_ref, bf16[512,3200]{1,0:T(8,128)(2,1)} %all-gather.2.cloned.1.call-done.dy_ref.p_ref, bf16[672,512]{1,0:T(8,128)(2,1)S(1)} %broadcast_dynamic-update-slice_fusion.others_ref, ...), custom_call_target="tpu_custom_call" | custom-call | flops 2113929216 | bytes 12000000 | tf_op jit(solution)/shard_map/down_parts/pallas_call | solution.py:113
  100.9 0.0 reduce-scatter.2.cloned.1.call-update
  100.9 5.6 %hidden_parts.1 = bf16[512,768]{1,0:T(8,128)(2,1)S(1)} custom-call(bf16[512,3200]{1,0:T(8,128)(2,1)} %all-gather.2.cloned.1.call-done.dy_ref.p_ref, bf16[512,3200]{1,0:T(8,128)(2,1)} %all-gather.2.cloned.1.call-done.dy_ref.p_ref, bf16[672,3072]{1,0:T(8,128)(2,1)} %constant_dynamic-update-slice_fusion.w_ref._, bf16[512,672]{1,0:T(8,128)(2,1)S(1)} %reshape.35.h_ref), custom_call_target="tpu_custom_call" | custom-call | flops 2113929216 | bytes 9000000 | tf_op jit(solution)/shard_map/hidden_parts/pallas_call | solution.py:167
  106.5 0.0 copy-start.3
  106.5 28.7 %all_to_all.21 = bf16[8,64,768]{2,1,0:T(8,128)(2,1)S(1)} all-to-all(bf16[8,64,768]{2,1,0:T(8,128)(2,1)S(1)} %bitcast.20), channel_id=1, replica_groups=mesh['y'=8,'x'=4,'expert'=16] {'y'}, dimensions={0} | all-to-all | bytes 1572864 | tf_op jit(solution)/shard_map/all_to_all | solution.py:249
  135.2 0.2 convert_reduce_fusion
  135.4 0.7 all_to_all.15
  136.1 3.5 %all-to-all-start.2 = ((f32[16,1,4]{2,1,0:T(1,128)}), f32[16,1,4]{2,1,0:T(1,128)S(1)}, u32[]{:S(2)}, u32[]{:S(2)}) async-start(f32[16,1,4]{2,1,0:T(1,128)} %bitcast.6), calls=%async_computation.2 | async-start | bytes 16384 | tf_op jit(solution)/shard_map/all_to_all | solution.py:254
  139.6 0.1 slice_bitcast_fusion
  139.6 0.4 copy.25
  140.1 1.9 %reshape.37 = bf16[1,1,16,4,5376]{4,3,2,1,0:T(4,128)(2,1)} reshape(bf16[64,8,672]{2,1,0:T(8,128)(2,1)S(1)} %copy.25) | data formatting | bytes 1376256 | tf_op jit(solution)/shard_map/reshape | solution.py:252
  141.9 5.1 %all-to-all-done.2 = f32[16,1,4]{2,1,0:T(1,128)S(1)} async-done(((f32[16,1,4]{2,1,0:T(1,128)}), f32[16,1,4]{2,1,0:T(1,128)S(1)}, u32[]{:S(2)}, u32[]{:S(2)}) %all-to-all-start.2) | async-done | bytes 288 | tf_op jit(solution)/shard_map/all_to_all | solution.py:254
  147.1 0.7 pick_probs.1
  147.8 2.8 %add_bitcast_fusion = f32[1,168,3072]{2,1,0:T(8,128)} fusion(f32[168,3072]{1,0:T(8,128)S(1)} %copy-done.3, bf16[168,3072]{1,0:T(8,128)(2,1)} %reduce-scatter.2.cloned.1.call-done), kind=kLoop, calls=%fused_computation | loop fusion | flops 1032192 | bytes 5160960 | tf_op jit(solution)/shard_map/reshape | solution.py:259
  (7 shorter events, 0.1 us)
Async XLA Ops:
  7.2 10.9 %copy-start.1 = (s32[8,4]{0,1:T(4,128)S(1)}, s32[8,4]{0,1:T(4,128)}, u32[]{:S(2)}) copy-start(s32[8,4]{0,1:T(4,128)} %param.6) | copy-start | bytes 388
  7.2 10.9 %copy-start = (bf16[8,3072]{1,0:T(8,128)(2,1)S(1)}, bf16[8,3072]{1,0:T(8,128)(2,1)}, u32[]{:S(2)}) copy-start(bf16[8,3072]{1,0:T(8,128)(2,1)} %dy_ref.1) | copy-start | bytes 147460
  7.2 10.9 %copy-start.2 = (bf16[8,4]{0,1:T(4,128)(2,1)S(1)}, bf16[8,4]{0,1:T(4,128)(2,1)}, u32[]{:S(2)}) copy-start(bf16[8,4]{0,1:T(4,128)(2,1)} %param.7) | copy-start | bytes 196
  7.2 37.6 %copy-start.4 = (bf16[1,168,3072]{2,1,0:T(8,128)(2,1)S(1)}, bf16[1,168,3072]{2,1,0:T(8,128)(2,1)}, u32[]{:S(2)}) copy-start(bf16[1,168,3072]{2,1,0:T(8,128)(2,1)} %param.9) | copy-start | bytes 3096580
  10.9 32.7 %all-to-all-start = ((bf16[8,16,4,672]{3,2,1,0:T(4,128)(2,1)}), bf16[8,16,4,672]{3,2,1,0:T(4,128)(2,1)S(1)}, u32[]{:S(2)}, u32[]{:S(2)}) async-start(bf16[8,16,4,672]{3,2,1,0:T(4,128)(2,1)} %bitcast.18), calls=%async_computation | async-start | bytes 1572864 | tf_op jit(solution)/shard_map/all_to_all | solution.py:233
  18.0 76.8 %all-gather.2.cloned.1.call-start = ((), (), s32[]{:S(2)}) async-start(), calls=%async_computation.4 | async-start | bytes 3686400 | tf_op jit(solution)/shard_map/all_gather | solution.py:237
  44.8 103.0 %reduce-scatter.2.cloned.1.call-start = ((), (), s32[]{:S(2)}) async-start(), calls=%async_computation.5 | async-start | bytes 5160960 | tf_op jit(solution)/shard_map/reduce_scatter | solution.py:245
  44.8 27.1 %collective-permute-start = (bf16[168,3072]{1,0:T(8,128)(2,1)S(1)}, bf16[168,3072]{1,0:T(8,128)(2,1)}, u32[]{:S(2)}, u32[]{:S(2)}) collective-permute-start(bf16[168,3072]{1,0:T(8,128)(2,1)S(1)} %bitcast.25), channel_id=1, source_target_pairs={{0,16},{16,32},{32,48},{48,0},{1,17},{17,33},{33,49},{49,1},{2,18}... | collective-permute-start | bytes 3096584 | tf_op jit(solution)/shard_map/ppermute | solution.py:19
  47.2 30.1 %collective-permute-start.1 = (bf16[168,3072]{1,0:T(8,128)(2,1)S(1)}, bf16[168,3072]{1,0:T(8,128)(2,1)S(1)}, u32[]{:S(2)}, u32[]{:S(2)}) collective-permute-start(bf16[168,3072]{1,0:T(8,128)(2,1)S(1)} %bitcast.26), channel_id=1, source_target_pairs={{0,48},{16,0},{32,16},{48,32},{1,49},{17,1},{33,17},{49,33},{2,50}... | collective-permute-start | bytes 3096584 | tf_op jit(solution)/shard_map/ppermute | solution.py:19
  73.8 14.8 %collective-permute-start.2 = (bf16[80,3072]{1,0:T(8,128)(2,1)}, bf16[80,3072]{1,0:T(8,128)(2,1)S(1)}, u32[]{:S(2)}, u32[]{:S(2)}) collective-permute-start(bf16[80,3072]{1,0:T(8,128)(2,1)} %slice.16), channel_id=1, source_target_pairs={{0,16},{16,32},{32,48},{48,0},{1,17},{17,33},{33,49},{49,1},{2,18}... | collective-permute-start | bytes 1474568 | tf_op jit(solution)/shard_map/ppermute | solution.py:19
  77.4 16.6 %collective-permute-start.3 = (bf16[88,3072]{1,0:T(8,128)(2,1)S(1)}, bf16[88,3072]{1,0:T(8,128)(2,1)S(1)}, u32[]{:S(2)}, u32[]{:S(2)}) collective-permute-start(bf16[88,3072]{1,0:T(8,128)(2,1)S(1)} %slice.17), channel_id=1, source_target_pairs={{0,48},{16,0},{32,16},{48,32},{1,49},{17,1},{33,17},{49,33},{2,50}... | collective-permute-start | bytes 1622024 | tf_op jit(solution)/shard_map/ppermute | solution.py:19
  106.5 41.3 %copy-start.3 = (f32[168,3072]{1,0:T(8,128)S(1)}, f32[168,3072]{1,0:T(8,128)}, u32[]{:S(2)}) copy-start(f32[168,3072]{1,0:T(8,128)} %get-tuple-element.5) | copy-start | bytes 6193156
  136.1 11.0 %all-to-all-start.2 = ((f32[16,1,4]{2,1,0:T(1,128)}), f32[16,1,4]{2,1,0:T(1,128)S(1)}, u32[]{:S(2)}, u32[]{:S(2)}) async-start(f32[16,1,4]{2,1,0:T(1,128)} %bitcast.6), calls=%async_computation.2 | async-start | bytes 16384 | tf_op jit(solution)/shard_map/all_to_all | solution.py:254
Sparse Core Ops, SparseCore 0:
  44.9 45.5 all-gather.1
  101.0 46.5 reduce-scatter.1

commit v4 on v3

--- a/solution.py
+++ b/solution.py
@@ -100,47 +100,44 @@
     )(me, gathered, after)
 
 
-def down_parts(every, h_others, h_own, after, width):
+def down_parts(every, h_others, after, width):
     rows = every.shape[0]
-    cols, share = h_others.shape[0], h_own.shape[0]
-
-    def kernel(dy_ref, p_ref, others_ref, mine_ref, _, out_ref, own_ref):
+    cols = h_others.shape[0]
+
+    def kernel(dy_ref, p_ref, others_ref, _, out_ref):
         g = (p_ref[:, :1].astype(F32) * dy_ref[...].astype(F32)).astype(BF16)
         out_ref[...] = jnp.dot(others_ref[...], g, preferred_element_type=F32).astype(BF16)
-        own_ref[...] = jnp.dot(mine_ref[...], g, preferred_element_type=F32)
 
     tile = lambda n: pl.BlockSpec((n, TILE), lambda i: (0, i))
     return pl.pallas_call(
         kernel,
         grid=(width // TILE,),
-        out_shape=(
-            jax.ShapeDtypeStruct((cols, width), BF16),
-            jax.ShapeDtypeStruct((share, width), F32),
-        ),
+        out_shape=jax.ShapeDtypeStruct((cols, width), BF16),
         in_specs=[
             tile(rows),
             pl.BlockSpec((rows, LANES), lambda i: (0, width // LANES)),
             pl.BlockSpec((cols, rows), lambda i: (0, 0)),
-            pl.BlockSpec((share, rows), lambda i: (0, 0)),
             pl.BlockSpec(memory_space=pl.ANY),
         ],
-        out_specs=(tile(cols), tile(share)),
+        out_specs=tile(cols),
         compiler_params=params(),
         cost_estimate=pl.CostEstimate(
             flops=2 * rows * cols * width, bytes_accessed=12000000, transcendentals=0
         ),
         name="down_parts",
-    )(every, every, h_others, h_own, after)
-
-
-def hidden_parts(every, w_cols, h, width, wide):
+    )(every, every, h_others, after)
+
+
+def hidden_parts(every, w_cols, h, h_own, width, wide):
     rows = every.shape[0]
-    cols = h.shape[1]
+    cols, share = h.shape[1], h_own.shape[0]
     steps = width // TILE
     edge = cols // LANES * LANES
 
-    def kernel(dy_ref, p_ref, w_ref, h_ref, out_ref, acc):
+    def kernel(dy_ref, p_ref, w_ref, h_ref, mine_ref, out_ref, own_ref, acc):
         step = pl.program_id(0)
+        g = (p_ref[:, :1].astype(F32) * dy_ref[...].astype(F32)).astype(BF16)
+        own_ref[...] = jnp.dot(mine_ref[...], g, preferred_element_type=F32)
         term = lax.dot_general(
             dy_ref[...], w_ref[...], (((1,), (1,)), ((), ())), preferred_element_type=F32
         )
@@ -167,21 +164,28 @@
     return pl.pallas_call(
         kernel,
         grid=(steps,),
-        out_shape=jax.ShapeDtypeStruct((rows, wide), BF16),
+        out_shape=(
+            jax.ShapeDtypeStruct((rows, wide), BF16),
+            jax.ShapeDtypeStruct((share, width), F32),
+        ),
         in_specs=[
             pl.BlockSpec((rows, TILE), lambda i: (0, i)),
             pl.BlockSpec((rows, LANES), lambda i: (0, width // LANES)),
             pl.BlockSpec((cols, TILE), lambda i: (0, i)),
             pl.BlockSpec((rows, cols), lambda i: (0, 0)),
+            pl.BlockSpec((share, rows), lambda i: (0, 0)),
         ],
-        out_specs=pl.BlockSpec((rows, wide), lambda i: (0, 0)),
+        out_specs=(
+            pl.BlockSpec((rows, wide), lambda i: (0, 0)),
+            pl.BlockSpec((share, TILE), lambda i: (0, i)),
+        ),
         scratch_shapes=[pltpu.VMEM((rows, wide), F32)],
         compiler_params=params(),
         cost_estimate=pl.CostEstimate(
             flops=2 * rows * cols * width, bytes_accessed=9000000, transcendentals=0
         ),
         name="hidden_parts",
-    )(every, every, w_cols, h)
+    )(every, every, w_cols, h, h_own)
 
 
 def pick_probs(routes, values):
@@ -241,11 +245,10 @@
     h_t = h.T
     h_own = lax.dynamic_slice(h_t, (x * share, 0), (share, YS * rows))
     h_others = lax.dynamic_update_slice(h_t, jnp.zeros_like(h_own), (x * share, 0))
-    others, own = down_parts(every, h_others, h_own, w_cols, width)
+    others = down_parts(every, h_others, w_cols, width)
     others = lax.psum_scatter(others, "x", scatter_dimension=0, tiled=True)
-    d_down = own + others.astype(F32)
-
-    back = hidden_parts(every, w_cols, h, width, wide)
+
+    back, own = hidden_parts(every, w_cols, h, h_own, width, wide)
     back = lax.all_to_all(
         back.reshape(YS, rows, wide), "y", split_axis=0, concat_axis=0, tiled=True
     )
@@ -256,6 +259,7 @@
     )
 
     d_probs = pick_probs(routes, returned.reshape(nexp, cap)).T
+    d_down = own + others.astype(F32)
     return d_probs, d_hidden, d_down.reshape(w_down.shape)
 
 

time: 161 us -> 160 us (level); the launches traced: 157 us -> 159 us
  transfers between devices with their start and end apart: 8 -> 8, of which waited for: 4 -> 4; matrix products, arithmetic and copies ran while one was open for 9% -> 9% of each run, Pallas kernels for 4% -> 5%
where the time goes in v4:
time: 160 us; the launch traced here: 159 us
  blocking collectives  54.1 us (34%)
  waiting for transfers between devices  31.2 us (20%)
  starting transfers between devices  22.3 us (14%)
  local copies, waits for them, and re-layouts  18.9 us (12%)
  Pallas kernels  14.9 us (9%)
  between operations  14.3 us (9%)
  other arithmetic  3 us (2%)
    all_to_all x1, blocking collectives, body(): lax.all_to_all(back.reshape(YS, rows, wide), 'y', split_axis=0, concat_ax...  28.7 us
    ppermute x4, waiting for transfers between devices, shift(): return lax.ppermute(a, 'x', [(i, (i + step) % XS) for i in range(XS)])  26 us
    all_gather x1, blocking collectives, body(): lax.all_gather(pack(grad_out, routes, probs, me.reshape(1)), 'expert', ax...  25.4 us
    ppermute x4, starting transfers between devices, shift(): return lax.ppermute(a, 'x', [(i, (i + step) % XS) for i in range(XS)])  11.7 us
    pallas_call x1, Pallas kernels, hidden_parts(): pl.pallas_call(kernel, grid=(steps,), out_shape=(jax.ShapeDtypeStruct((ro...  7.39 us
    all_to_all x1, starting transfers between devices, body(): h = lax.all_to_all(h, 'y', split_axis=0, concat_axis=0, tiled=True)  7.1 us
    dynamic_update_slice x5, local copies, waits for them, and re-layouts, gather_w(): lax.dynamic_update_slice(o, v, ((x + step) % XS * n + low, 0))  7.08 us
    pallas_call x1, Pallas kernels, down_parts(): pl.pallas_call(kernel, grid=(width // TILE,), out_shape=jax.ShapeDtypeStr...  5.5 us
  transfers between devices with their start and end apart: 8, of which 4 were waited for; matrix products, arithmetic and copies ran while one was open for 9% of the time, Pallas kernels for 5%

profile of v4, /device:TPU:6, one launch (start us, length us, event | category | flops | bytes accessed | tf_op | source)
XLA Modules:
  0.0 158.6 jit_solution(15459425703791990836)
XLA Ops:
  7.2 0.0 copy-start.1
  7.2 0.0 copy-start.2
  7.2 0.0 copy-start
  7.2 0.0 copy-start.4
  7.2 2.5 %reshape.39 = bf16[16,4,8,672]{3,2,1,0:T(8,128)(2,1)S(1)} reshape(bf16[1,1,16,4,5376]{4,3,2,1,0:T(4,128)(2,1)} %param.8) | data formatting | bytes 1376256 | tf_op jit(solution)/shard_map/reshape | solution.py:236
  9.7 1.2 copy.32
  10.9 7.1 %all-to-all-start = ((bf16[8,16,4,672]{3,2,1,0:T(4,128)(2,1)}), bf16[8,16,4,672]{3,2,1,0:T(4,128)(2,1)S(1)}, u32[]{:S(2)}, u32[]{:S(2)}) async-start(bf16[8,16,4,672]{3,2,1,0:T(4,128)(2,1)} %bitcast.18), calls=%async_computation | async-start | bytes 1572864 | tf_op jit(solution)/shard_map/all_to_all | solution.py:237
  18.0 0.0 all-gather.2.cloned.1.call-start
  18.1 0.0 copy-done.1
  18.1 0.0 copy-done.2
  18.1 0.0 copy-done
  18.1 0.1 pack_tokens.1
  18.2 25.4 %all_gather.6.refs_1_ = bf16[128,3200]{1,0:T(8,128)(2,1)S(1)} all-gather(bf16[8,3200]{1,0:T(8,128)(2,1)S(1)} %pack_tokens.1), channel_id=1, replica_groups=mesh['y'=8,'x'=4,'expert'=16] {'expert'}, dimensions={0}, use_global_device_ids=true | all-gather | bytes 870400 | tf_op jit(solution)/shard_map/all_gather | solution.py:239
  43.6 0.0 all-to-all-done.refs_2_
  43.6 1.2 pick_slots.1
  44.8 0.0 all-gather.2.cloned.1.call-update
  44.8 0.0 reduce-scatter.2.cloned.1.call-start
  44.8 0.0 copy-done.4
  44.8 2.4 %collective-permute-start = (bf16[168,3072]{1,0:T(8,128)(2,1)S(1)}, bf16[168,3072]{1,0:T(8,128)(2,1)}, u32[]{:S(2)}, u32[]{:S(2)}) collective-permute-start(bf16[168,3072]{1,0:T(8,128)(2,1)S(1)} %bitcast.25), channel_id=1, source_target_pairs={{0,16},{16,32},{32,48},{48,0},{1,17},{17,33},{33,49},{49,1},{2,18}... | collective-permute-start | bytes 3096584 | tf_op jit(solution)/shard_map/ppermute | solution.py:19
  47.2 3.5 %collective-permute-start.1 = (bf16[168,3072]{1,0:T(8,128)(2,1)S(1)}, bf16[168,3072]{1,0:T(8,128)(2,1)S(1)}, u32[]{:S(2)}, u32[]{:S(2)}) collective-permute-start(bf16[168,3072]{1,0:T(8,128)(2,1)S(1)} %bitcast.26), channel_id=1, source_target_pairs={{0,48},{16,0},{32,16},{48,32},{1,49},{17,1},{33,17},{49,33},{2,50}... | collective-permute-start | bytes 3096584 | tf_op jit(solution)/shard_map/ppermute | solution.py:19
  50.8 2.5 %broadcast_in_dim.6 = bf16[672,3072]{1,0:T(8,128)(2,1)} broadcast(bf16[]{:T(256)} %constant.42.clone.1), dimensions={} | broadcast | bytes 4128770 | tf_op jit(solution)/shard_map/broadcast_in_dim | solution.py:27
  53.2 1.1 constant_dynamic-update-slice_fusion.4
  54.3 17.6 %collective-permute-done = bf16[168,3072]{1,0:T(8,128)(2,1)} collective-permute-done((bf16[168,3072]{1,0:T(8,128)(2,1)S(1)}, bf16[168,3072]{1,0:T(8,128)(2,1)}, u32[]{:S(2)}, u32[]{:S(2)}) %collective-permute-start) | collective-permute-done | bytes 1032224 | tf_op jit(solution)/shard_map/ppermute | solution.py:19
  71.9 1.8 %slice.16 = bf16[80,3072]{1,0:T(8,128)(2,1)} slice(bf16[168,3072]{1,0:T(8,128)(2,1)} %collective-permute-done), slice={[0:80], [0:3072]} | slice | bytes 983040 | tf_op jit(solution)/shard_map/slice | solution.py:26
  73.8 3.6 %collective-permute-start.2 = (bf16[80,3072]{1,0:T(8,128)(2,1)}, bf16[80,3072]{1,0:T(8,128)(2,1)}, u32[]{:S(2)}, u32[]{:S(2)}) collective-permute-start(bf16[80,3072]{1,0:T(8,128)(2,1)} %slice.16), channel_id=1, source_target_pairs={{0,16},{16,32},{32,48},{48,0},{1,17},{17,33},{33,49},{49,1},{2,18}... | collective-permute-start | bytes 1474568 | tf_op jit(solution)/shard_map/ppermute | solution.py:19
  77.4 0.0 collective-permute-done.1
  77.4 2.2 %collective-permute-start.3 = (bf16[88,3072]{1,0:T(8,128)(2,1)S(1)}, bf16[88,3072]{1,0:T(8,128)(2,1)S(1)}, u32[]{:S(2)}, u32[]{:S(2)}) collective-permute-start(bf16[88,3072]{1,0:T(8,128)(2,1)S(1)} %slice.17), channel_id=1, source_target_pairs={{0,48},{16,0},{32,16},{48,32},{1,49},{17,1},{33,17},{49,33},{2,50}... | collective-permute-start | bytes 1622024 | tf_op jit(solution)/shard_map/ppermute | solution.py:19
  79.7 2.3 %constant_dynamic-update-slice_fusion.3 = bf16[672,3072]{1,0:T(8,128)(2,1)} fusion(bf16[672,3072]{1,0:T(8,128)(2,1)} %constant_dynamic-update-slice_fusion.4, bf16[168,3072]{1,0:T(8,128)(2,1)} %collective-permute-done, s32[]{:T(128)S(6)} %select_n.43), kind=kLoop, calls=%fused_computation.9 | loop fusion | bytes 2064388 | tf_op jit(solution)/shard_map/dynamic_update_slice | solution.py:28
  82.0 1.0 constant_dynamic-update-slice_fusion.2
  83.0 0.4 reshape.35.h_ref
  83.4 0.3 copy.22
  83.7 4.9 %collective-permute-done.2 = bf16[80,3072]{1,0:T(8,128)(2,1)} collective-permute-done((bf16[80,3072]{1,0:T(8,128)(2,1)}, bf16[80,3072]{1,0:T(8,128)(2,1)}, u32[]{:S(2)}, u32[]{:S(2)}) %collective-permute-start.2) | collective-permute-done | bytes 491552 | tf_op jit(solution)/shard_map/ppermute | solution.py:19
  88.6 1.9 %constant_dynamic-update-slice_fusion.1 = bf16[672,3072]{1,0:T(8,128)(2,1)} fusion(bf16[672,3072]{1,0:T(8,128)(2,1)} %constant_dynamic-update-slice_fusion.2, bf16[80,3072]{1,0:T(8,128)(2,1)} %collective-permute-done.2, s32[]{:T(128)S(6)} %select_n.47), kind=kLoop, calls=%fused_computation.7 | loop fusion | bytes 983044 | tf_op jit(solution)/shard_map/dynamic_update_slice | solution.py:28
  90.5 3.5 %collective-permute-done.3 = bf16[88,3072]{1,0:T(8,128)(2,1)S(1)} collective-permute-done((bf16[88,3072]{1,0:T(8,128)(2,1)S(1)}, bf16[88,3072]{1,0:T(8,128)(2,1)S(1)}, u32[]{:S(2)}, u32[]{:S(2)}) %collective-permute-start.3) | collective-permute-done | bytes 540704 | tf_op jit(solution)/shard_map/ppermute | solution.py:19
  94.0 0.8 constant_dynamic-update-slice_fusion.w_ref._
  94.8 5.5 %down_parts.1 = bf16[672,3072]{1,0:T(8,128)(2,1)} custom-call(bf16[512,3200]{1,0:T(8,128)(2,1)} %all-gather.2.cloned.1.call-done.dy_ref.p_ref, bf16[512,3200]{1,0:T(8,128)(2,1)} %all-gather.2.cloned.1.call-done.dy_ref.p_ref, bf16[672,512]{1,0:T(8,128)(2,1)S(1)} %broadcast_dynamic-update-slice_fusion.others_ref, ...), custom_call_target="tpu_custom_call" | custom-call | flops 2113929216 | bytes 12000000 | tf_op jit(solution)/shard_map/down_parts/pallas_call | solution.py:112
  100.3 0.0 reduce-scatter.2.cloned.1.call-update
  100.3 7.4 %hidden_parts.1 = (bf16[512,768]{1,0:T(8,128)(2,1)S(1)}, f32[168,3072]{1,0:T(8,128)}) custom-call(bf16[512,3200]{1,0:T(8,128)(2,1)} %all-gather.2.cloned.1.call-done.dy_ref.p_ref, bf16[512,3200]{1,0:T(8,128)(2,1)} %all-gather.2.cloned.1.call-done.dy_ref.p_ref, bf16[672,3072]{1,0:T(8,128)(2,1)} %constant_dynamic-update-slice_fusion.w_ref._, ...), custom_call_target="tpu_custom_call" | custom-call | flops 2113929216 | bytes 9000000 | tf_op jit(solution)/shard_map/hidden_parts/pallas_call | solution.py:164
  107.7 28.7 %all_to_all.21 = bf16[8,64,768]{2,1,0:T(8,128)(2,1)S(1)} all-to-all(bf16[8,64,768]{2,1,0:T(8,128)(2,1)S(1)} %bitcast.20), channel_id=1, replica_groups=mesh['y'=8,'x'=4,'expert'=16] {'y'}, dimensions={0} | all-to-all | bytes 1572864 | tf_op jit(solution)/shard_map/all_to_all | solution.py:252
  136.4 0.2 convert_reduce_fusion
  136.6 0.7 all_to_all.15
  137.3 3.5 %all-to-all-start.2 = ((f32[16,1,4]{2,1,0:T(1,128)}), f32[16,1,4]{2,1,0:T(1,128)S(1)}, u32[]{:S(2)}, u32[]{:S(2)}) async-start(f32[16,1,4]{2,1,0:T(1,128)} %bitcast.7), calls=%async_computation.2 | async-start | bytes 16384 | tf_op jit(solution)/shard_map/all_to_all | solution.py:257
  140.8 0.1 slice_bitcast_fusion
  140.8 0.4 copy.26
  141.3 1.9 %reshape.37 = bf16[1,1,16,4,5376]{4,3,2,1,0:T(4,128)(2,1)} reshape(bf16[64,8,672]{2,1,0:T(8,128)(2,1)S(1)} %copy.26) | data formatting | bytes 1376256 | tf_op jit(solution)/shard_map/reshape | solution.py:255
  143.1 5.1 %all-to-all-done.2 = f32[16,1,4]{2,1,0:T(1,128)S(1)} async-done(((f32[16,1,4]{2,1,0:T(1,128)}), f32[16,1,4]{2,1,0:T(1,128)S(1)}, u32[]{:S(2)}, u32[]{:S(2)}) %all-to-all-start.2) | async-done | bytes 288 | tf_op jit(solution)/shard_map/all_to_all | solution.py:257
  148.3 0.7 pick_probs.1
  149.0 2.8 %add_bitcast_fusion = f32[1,168,3072]{2,1,0:T(8,128)} fusion(f32[168,3072]{1,0:T(8,128)S(1)} %copy-done.3, bf16[168,3072]{1,0:T(8,128)(2,1)} %reduce-scatter.2.cloned.1.call-done), kind=kLoop, calls=%fused_computation | loop fusion | flops 1032192 | bytes 5160960 | tf_op jit(solution)/shard_map/reshape | solution.py:263
  (7 shorter events, 0.1 us)
Async XLA Ops:
  7.2 10.9 %copy-start.1 = (s32[8,4]{0,1:T(4,128)S(1)}, s32[8,4]{0,1:T(4,128)}, u32[]{:S(2)}) copy-start(s32[8,4]{0,1:T(4,128)} %param.6) | copy-start | bytes 388
  7.2 10.9 %copy-start.2 = (bf16[8,4]{0,1:T(4,128)(2,1)S(1)}, bf16[8,4]{0,1:T(4,128)(2,1)}, u32[]{:S(2)}) copy-start(bf16[8,4]{0,1:T(4,128)(2,1)} %param.7) | copy-start | bytes 196
  7.2 10.9 %copy-start = (bf16[8,3072]{1,0:T(8,128)(2,1)S(1)}, bf16[8,3072]{1,0:T(8,128)(2,1)}, u32[]{:S(2)}) copy-start(bf16[8,3072]{1,0:T(8,128)(2,1)} %dy_ref.1) | copy-start | bytes 147460
  7.2 37.6 %copy-start.4 = (bf16[1,168,3072]{2,1,0:T(8,128)(2,1)S(1)}, bf16[1,168,3072]{2,1,0:T(8,128)(2,1)}, u32[]{:S(2)}) copy-start(bf16[1,168,3072]{2,1,0:T(8,128)(2,1)} %param.9) | copy-start | bytes 3096580
  10.9 32.7 %all-to-all-start = ((bf16[8,16,4,672]{3,2,1,0:T(4,128)(2,1)}), bf16[8,16,4,672]{3,2,1,0:T(4,128)(2,1)S(1)}, u32[]{:S(2)}, u32[]{:S(2)}) async-start(bf16[8,16,4,672]{3,2,1,0:T(4,128)(2,1)} %bitcast.18), calls=%async_computation | async-start | bytes 1572864 | tf_op jit(solution)/shard_map/all_to_all | solution.py:237
  18.0 76.8 %all-gather.2.cloned.1.call-start = ((), (), s32[]{:S(2)}) async-start(), calls=%async_computation.4 | async-start | bytes 3686400 | tf_op jit(solution)/shard_map/all_gather | solution.py:241
  44.8 104.2 %reduce-scatter.2.cloned.1.call-start = ((), (), s32[]{:S(2)}) async-start(), calls=%async_computation.5 | async-start | bytes 5160960 | tf_op jit(solution)/shard_map/reduce_scatter | solution.py:249
  44.8 27.1 %collective-permute-start = (bf16[168,3072]{1,0:T(8,128)(2,1)S(1)}, bf16[168,3072]{1,0:T(8,128)(2,1)}, u32[]{:S(2)}, u32[]{:S(2)}) collective-permute-start(bf16[168,3072]{1,0:T(8,128)(2,1)S(1)} %bitcast.25), channel_id=1, source_target_pairs={{0,16},{16,32},{32,48},{48,0},{1,17},{17,33},{33,49},{49,1},{2,18}... | collective-permute-start | bytes 3096584 | tf_op jit(solution)/shard_map/ppermute | solution.py:19
  47.2 30.1 %collective-permute-start.1 = (bf16[168,3072]{1,0:T(8,128)(2,1)S(1)}, bf16[168,3072]{1,0:T(8,128)(2,1)S(1)}, u32[]{:S(2)}, u32[]{:S(2)}) collective-permute-start(bf16[168,3072]{1,0:T(8,128)(2,1)S(1)} %bitcast.26), channel_id=1, source_target_pairs={{0,48},{16,0},{32,16},{48,32},{1,49},{17,1},{33,17},{49,33},{2,50}... | collective-permute-start | bytes 3096584 | tf_op jit(solution)/shard_map/ppermute | solution.py:19
  73.8 14.9 %collective-permute-start.2 = (bf16[80,3072]{1,0:T(8,128)(2,1)}, bf16[80,3072]{1,0:T(8,128)(2,1)}, u32[]{:S(2)}, u32[]{:S(2)}) collective-permute-start(bf16[80,3072]{1,0:T(8,128)(2,1)} %slice.16), channel_id=1, source_target_pairs={{0,16},{16,32},{32,48},{48,0},{1,17},{17,33},{33,49},{49,1},{2,18}... | collective-permute-start | bytes 1474568 | tf_op jit(solution)/shard_map/ppermute | solution.py:19
  77.4 16.5 %collective-permute-start.3 = (bf16[88,3072]{1,0:T(8,128)(2,1)S(1)}, bf16[88,3072]{1,0:T(8,128)(2,1)S(1)}, u32[]{:S(2)}, u32[]{:S(2)}) collective-permute-start(bf16[88,3072]{1,0:T(8,128)(2,1)S(1)} %slice.17), channel_id=1, source_target_pairs={{0,48},{16,0},{32,16},{48,32},{1,49},{17,1},{33,17},{49,33},{2,50}... | collective-permute-start | bytes 1622024 | tf_op jit(solution)/shard_map/ppermute | solution.py:19
  107.7 41.3 %copy-start.3 = (f32[168,3072]{1,0:T(8,128)S(1)}, f32[168,3072]{1,0:T(8,128)}, u32[]{:S(2)}) copy-start(f32[168,3072]{1,0:T(8,128)} %get-tuple-element.6) | copy-start | bytes 6193156
  137.3 11.0 %all-to-all-start.2 = ((f32[16,1,4]{2,1,0:T(1,128)}), f32[16,1,4]{2,1,0:T(1,128)S(1)}, u32[]{:S(2)}, u32[]{:S(2)}) async-start(f32[16,1,4]{2,1,0:T(1,128)} %bitcast.7), calls=%async_computation.2 | async-start | bytes 16384 | tf_op jit(solution)/shard_map/all_to_all | solution.py:257
Sparse Core Ops, SparseCore 0:
  44.9 45.5 all-gather.1
  100.4 46.5 reduce-scatter.1
